TPU v7x, 512 devices: a whole 4x8x8 slice. The times are simulated.
512 devices in a mesh: section: 32 (over z, y_hi), tensor: 16 (over x, y_lo, core).
Axes of the slice: x: 4, y: 8 (y_hi: 4, y_lo: 2; y = y_hi * 2 + y_lo), z: 8, core: 2. Of those that a mesh axis runs over, the one named last changes fastest.
Arguments:
- down_batch_input: bfloat16 [8, 64, 4096], P(None, None, 'tensor'), may hold values from -6 to 6
- up_batch_input: bfloat16 [8, 64, 4096], P(None, None, 'tensor'), may hold values from -6 to 6
- down_relay_lower_weight: bfloat16 [32, 4096, 64], P('section', 'tensor'), may hold values from -0.09375 to 0.09375
- down_relay_upper_weight: bfloat16 [32, 64, 4096], P('section', None, 'tensor'), may hold values from -0.1875 to 0.1875
- up_relay_lower_weight: bfloat16 [32, 4096, 64], P('section', 'tensor'), may hold values from -0.09375 to 0.09375
- up_relay_upper_weight: bfloat16 [32, 64, 4096], P('section', None, 'tensor'), may hold values from -0.1875 to 0.1875
- frozen_down_weight: bfloat16 [32, 4096, 4096], P('section', None, 'tensor'), may hold values from -0.046875 to 0.046875
- frozen_up_weight: bfloat16 [32, 4096, 4096], P('section', None, 'tensor'), may hold values from -0.046875 to 0.046875
Outputs:
- grad_a_down: float32 [32, 4096, 64], P('section', 'tensor')
- grad_b_down: float32 [32, 64, 4096], P('section', None, 'tensor')
- grad_a_up: float32 [32, 4096, 64], P('section', 'tensor')
- grad_b_up: float32 [32, 64, 4096], P('section', None, 'tensor')
All inputs are finite; a program needn't handle non-finite values.
Results may differ from a plain program's by a relative error of at most 0.014.
Values may be sent and summed in bfloat16 or wider, within the bound.
A program may use at most 64 MiB of HBM per device.

v0:
```python
import jax
import jax.numpy as jnp
from jax import lax
from jax.sharding import PartitionSpec as P

RELAY_LAYERS = 4


SCALE = 2.0


def from_behind(value, axis, steps):
    count = lax.axis_size(axis)
    leading, last = (max(0, -steps), min(count, count - steps))
    return lax.ppermute(value, axis, [(source, source + steps) for source in range(leading, last)])


def partial_coeff(hidden_state, a):
    return SCALE * jnp.dot(hidden_state, a, preferred_element_type=jnp.float32)


def finish_layer(hidden_state, base, c, b):
    out = (
        hidden_state.astype(jnp.float32) + base + jnp.dot(c, b, preferred_element_type=jnp.float32)
    )
    return out.astype(jnp.bfloat16)


def back_local(hidden_state, c, error_signal, g, across, a):
    grad_a = SCALE * jnp.dot(hidden_state.T, g, preferred_element_type=jnp.float32)
    grad_b = jnp.dot(c.T, error_signal, preferred_element_type=jnp.float32)
    e_prev = (
        error_signal.astype(jnp.float32)
        + across
        + SCALE * jnp.dot(g, a.T, preferred_element_type=jnp.float32)
    )
    return (e_prev.astype(jnp.bfloat16), grad_a, grad_b)


def body(
    down_batch_input,
    up_batch_input,
    down_relay_lower_weight,
    down_relay_upper_weight,
    up_relay_lower_weight,
    up_relay_upper_weight,
    frozen_down_weight,
    frozen_up_weight,
):
    position = lax.axis_index("section")
    local = position % RELAY_LAYERS
    group = position // RELAY_LAYERS
    down_adapter_lower, down_adapter_upper = (
        down_relay_lower_weight[0],
        down_relay_upper_weight[0],
    )
    up_adapter_lower, up_adapter_upper = (up_relay_lower_weight[0], up_relay_upper_weight[0])
    columns_down, columns_up = (frozen_down_weight[0], frozen_up_weight[0])
    rank = down_adapter_lower.shape[1]
    start_down = lax.dynamic_index_in_dim(down_batch_input, group, 0, keepdims=False)
    start_up = lax.dynamic_index_in_dim(up_batch_input, group, 0, keepdims=False)
    tokens, width = start_down.shape
    empty_c = jnp.zeros((tokens, rank), jnp.bfloat16)

    def forward_step(step, carry):
        buf_down, buf_up, save_down, save_up, keep_down, keep_up, last_down, last_up = carry
        sum_down, sum_up = lax.psum(
            (partial_coeff(buf_down, down_adapter_lower), partial_coeff(buf_up, up_adapter_lower)),
            "tensor",
        )
        c_down = sum_down.astype(jnp.bfloat16)
        c_up = sum_up.astype(jnp.bfloat16)
        based_down = jnp.dot(
            lax.all_gather(buf_down, "tensor", axis=1, tiled=True),
            columns_down,
            preferred_element_type=jnp.float32,
        )
        based_up = jnp.dot(
            lax.all_gather(buf_up, "tensor", axis=1, tiled=True),
            columns_up,
            preferred_element_type=jnp.float32,
        )
        active_down = local == step
        active_up = local == RELAY_LAYERS - 1 - step
        save_down = jnp.where(active_down, buf_down, save_down)
        save_up = jnp.where(active_up, buf_up, save_up)
        keep_down = jnp.where(active_down, c_down, keep_down)
        keep_up = jnp.where(active_up, c_up, keep_up)
        out_down = finish_layer(buf_down, based_down, c_down, down_adapter_upper)
        out_up = finish_layer(buf_up, based_up, c_up, up_adapter_upper)
        last_down = jnp.where(active_down, out_down, last_down)
        last_up = jnp.where(active_up, out_up, last_up)
        buf_down = from_behind(out_down, "section", 1)
        buf_up = from_behind(out_up, "section", -1)
        return (buf_down, buf_up, save_down, save_up, keep_down, keep_up, last_down, last_up)

    init = (start_down, start_up, start_down, start_up, empty_c, empty_c, start_down, start_up)
    carry = lax.fori_loop(0, RELAY_LAYERS, forward_step, init)
    save_down, save_up, coeff_down, coeff_up, last_down, last_up = (
        carry[2],
        carry[3],
        carry[4],
        carry[5],
        carry[6],
        carry[7],
    )
    groups_t = lax.axis_size("tensor")
    zero_a = jnp.zeros(down_adapter_lower.shape, jnp.float32)
    zero_b = jnp.zeros(down_adapter_upper.shape, jnp.float32)

    def backward_step(step, carry):
        e_down, e_up, ga_down, gb_down, ga_up, gb_up = carry
        g_down, g_up = lax.psum(
            (
                jnp.dot(e_down, down_adapter_upper.T, preferred_element_type=jnp.float32),
                jnp.dot(e_up, up_adapter_upper.T, preferred_element_type=jnp.float32),
            ),
            "tensor",
        )
        g_down = g_down.astype(jnp.bfloat16)
        g_up = g_up.astype(jnp.bfloat16)
        terms_down = jnp.dot(e_down, columns_down.T, preferred_element_type=jnp.float32)
        terms_up = jnp.dot(e_up, columns_up.T, preferred_element_type=jnp.float32)
        moved_down, moved_up = (
            lax.all_to_all(terms_down, "tensor", split_axis=1, concat_axis=0, tiled=True),
            lax.all_to_all(terms_up, "tensor", split_axis=1, concat_axis=0, tiled=True),
        )
        across_down = jnp.sum(moved_down.reshape(groups_t, tokens, width), axis=0)
        across_up = jnp.sum(moved_up.reshape(groups_t, tokens, width), axis=0)
        prev_down, da_down, db_down = back_local(
            save_down, coeff_down, e_down, g_down, across_down, down_adapter_lower
        )
        prev_up, da_up, db_up = back_local(
            save_up, coeff_up, e_up, g_up, across_up, up_adapter_lower
        )
        active_down = local == RELAY_LAYERS - 1 - step
        active_up = local == step
        ga_down = jnp.where(active_down, da_down, ga_down)
        gb_down = jnp.where(active_down, db_down, gb_down)
        ga_up = jnp.where(active_up, da_up, ga_up)
        gb_up = jnp.where(active_up, db_up, gb_up)
        e_down = from_behind(prev_down, "section", -1)
        e_up = from_behind(prev_up, "section", 1)
        return (e_down, e_up, ga_down, gb_down, ga_up, gb_up)

    result = lax.fori_loop(
        0, RELAY_LAYERS, backward_step, (last_down, last_up, zero_a, zero_b, zero_a, zero_b)
    )
    return (result[2][None], result[3][None], result[4][None], result[5][None])


def solution(mesh):
    in_specs = (
        P(None, None, "tensor"),
        P(None, None, "tensor"),
        P("section", "tensor", None),
        P("section", None, "tensor"),
        P("section", "tensor", None),
        P("section", None, "tensor"),
        P("section", None, "tensor"),
        P("section", None, "tensor"),
    )
    out_specs = (
        P("section", "tensor", None),
        P("section", None, "tensor"),
        P("section", "tensor", None),
        P("section", None, "tensor"),
    )
    return jax.shard_map(body, mesh=mesh, in_specs=in_specs, out_specs=out_specs, check_vma=False)
```

profile of v0, /device:TPU:1, one launch (start us, length us, event | category | flops | bytes accessed | tf_op | source)
XLA Modules:
  0.0 842.3 jit_solution(14853679713092410976)
XLA Ops:
  3.3 423.8 %while.52 = (s32[]{:T(128)}, bf16[64,256]{1,0:T(8,128)(2,1)S(1)}, bf16[64,256]{1,0:T(8,128)(2,1)S(1)}, bf16[64,256]{1,0:T(8,128)(2,1)S(1)}, bf16[64,256]{1,0:T(8...) while((s32[]{:T(128)}, bf16[64,256]{1,0:T(8,128)(2,1)S(1)}, ...), condition=%wide.region_3.4_spmd.clone, body=%wide.region_0.3_spmd.clone.sunk | while | flops 277053440 | bytes 16466303 | solution.py:98
  3.3 25.8 %all_gather.19 = bf16[64,4096]{1,0:T(8,128)(2,1)S(1)} all-gather(bf16[64,256]{1,0:T(8,128)(2,1)S(1)} %get-tuple-element.1011), channel_id=1, replica_groups=mesh['section'=32,'tensor'=16] {'tensor'}, dimensions={1}, use_global_device_ids=true | all-gather | bytes 557056 | tf_op jit(solution)/shard_map/while/body/eval_jaxpr/all_gather | solution.py:79
  29.4 49.9 %all-reduce.4 = (bf16[64,64]{1,0:T(8,128)(2,1)S(1)}, bf16[64,64]{1,0:T(8,128)(2,1)S(1)}) all-reduce(f32[64,64]{1,0:T(8,128)S(1)} %convolution_multiply_fusion.8, f32[64,64]{1,0:T(8,128)S(1)} %convolution_multiply_fusion.9), channel_id=1, replica_groups=mesh['section'=32,'tensor'=16] {'tensor'}, use_global_device_ids=true, to_apply=%region_1.1 | all-reduce | flops 8192 | bytes 49152 | tf_op jit(solution)/shard_map/while/body/eval_jaxpr/psum | solution.py:67
  79.3 2.0 convolution_add_fusion.7
  81.5 1.3 collective-permute-start.1
  82.8 23.2 %all_gather.18 = bf16[64,4096]{1,0:T(8,128)(2,1)S(1)} all-gather(bf16[64,256]{1,0:T(8,128)(2,1)S(1)} %get-tuple-element.1010), channel_id=1, replica_groups=mesh['section'=32,'tensor'=16] {'tensor'}, dimensions={1}, use_global_device_ids=true | all-gather | bytes 557056 | tf_op jit(solution)/shard_map/while/body/eval_jaxpr/all_gather | solution.py:74
  106.6 5.2 collective-permute-start
  112.8 20.4 %all_gather.19 = bf16[64,4096]{1,0:T(8,128)(2,1)S(1)} all-gather(bf16[64,256]{1,0:T(8,128)(2,1)S(1)} %get-tuple-element.1011), channel_id=1, replica_groups=mesh['section'=32,'tensor'=16] {'tensor'}, dimensions={1}, use_global_device_ids=true | all-gather | bytes 557056 | tf_op jit(solution)/shard_map/while/body/eval_jaxpr/all_gather | solution.py:79
  133.5 49.6 %all-reduce.4 = (bf16[64,64]{1,0:T(8,128)(2,1)S(1)}, bf16[64,64]{1,0:T(8,128)(2,1)S(1)}) all-reduce(f32[64,64]{1,0:T(8,128)S(1)} %convolution_multiply_fusion.8, f32[64,64]{1,0:T(8,128)S(1)} %convolution_multiply_fusion.9), channel_id=1, replica_groups=mesh['section'=32,'tensor'=16] {'tensor'}, use_global_device_ids=true, to_apply=%region_1.1 | all-reduce | flops 8192 | bytes 49152 | tf_op jit(solution)/shard_map/while/body/eval_jaxpr/psum | solution.py:67
  183.1 2.0 convolution_add_fusion.7
  185.4 1.3 collective-permute-start.1
  186.7 23.2 %all_gather.18 = bf16[64,4096]{1,0:T(8,128)(2,1)S(1)} all-gather(bf16[64,256]{1,0:T(8,128)(2,1)S(1)} %get-tuple-element.1010), channel_id=1, replica_groups=mesh['section'=32,'tensor'=16] {'tensor'}, dimensions={1}, use_global_device_ids=true | all-gather | bytes 557056 | tf_op jit(solution)/shard_map/while/body/eval_jaxpr/all_gather | solution.py:74
  210.5 5.3 collective-permute-start
  216.8 20.6 %all_gather.19 = bf16[64,4096]{1,0:T(8,128)(2,1)S(1)} all-gather(bf16[64,256]{1,0:T(8,128)(2,1)S(1)} %get-tuple-element.1011), channel_id=1, replica_groups=mesh['section'=32,'tensor'=16] {'tensor'}, dimensions={1}, use_global_device_ids=true | all-gather | bytes 557056 | tf_op jit(solution)/shard_map/while/body/eval_jaxpr/all_gather | solution.py:79
  237.7 49.3 %all-reduce.4 = (bf16[64,64]{1,0:T(8,128)(2,1)S(1)}, bf16[64,64]{1,0:T(8,128)(2,1)S(1)}) all-reduce(f32[64,64]{1,0:T(8,128)S(1)} %convolution_multiply_fusion.8, f32[64,64]{1,0:T(8,128)S(1)} %convolution_multiply_fusion.9), channel_id=1, replica_groups=mesh['section'=32,'tensor'=16] {'tensor'}, use_global_device_ids=true, to_apply=%region_1.1 | all-reduce | flops 8192 | bytes 49152 | tf_op jit(solution)/shard_map/while/body/eval_jaxpr/psum | solution.py:67
  287.0 2.0 convolution_add_fusion.7
  289.2 1.3 collective-permute-start.1
  290.5 23.2 %all_gather.18 = bf16[64,4096]{1,0:T(8,128)(2,1)S(1)} all-gather(bf16[64,256]{1,0:T(8,128)(2,1)S(1)} %get-tuple-element.1010), channel_id=1, replica_groups=mesh['section'=32,'tensor'=16] {'tensor'}, dimensions={1}, use_global_device_ids=true | all-gather | bytes 557056 | tf_op jit(solution)/shard_map/while/body/eval_jaxpr/all_gather | solution.py:74
  314.4 6.5 collective-permute-start
  321.9 21.2 %all_gather.19 = bf16[64,4096]{1,0:T(8,128)(2,1)S(1)} all-gather(bf16[64,256]{1,0:T(8,128)(2,1)S(1)} %get-tuple-element.1011), channel_id=1, replica_groups=mesh['section'=32,'tensor'=16] {'tensor'}, dimensions={1}, use_global_device_ids=true | all-gather | bytes 557056 | tf_op jit(solution)/shard_map/while/body/eval_jaxpr/all_gather | solution.py:79
  343.3 49.0 %all-reduce.4 = (bf16[64,64]{1,0:T(8,128)(2,1)S(1)}, bf16[64,64]{1,0:T(8,128)(2,1)S(1)}) all-reduce(f32[64,64]{1,0:T(8,128)S(1)} %convolution_multiply_fusion.8, f32[64,64]{1,0:T(8,128)S(1)} %convolution_multiply_fusion.9), channel_id=1, replica_groups=mesh['section'=32,'tensor'=16] {'tensor'}, use_global_device_ids=true, to_apply=%region_1.1 | all-reduce | flops 8192 | bytes 49152 | tf_op jit(solution)/shard_map/while/body/eval_jaxpr/psum | solution.py:67
  392.4 2.0 convolution_add_fusion.7
  394.6 1.3 collective-permute-start.1
  395.9 23.2 %all_gather.18 = bf16[64,4096]{1,0:T(8,128)(2,1)S(1)} all-gather(bf16[64,256]{1,0:T(8,128)(2,1)S(1)} %get-tuple-element.1010), channel_id=1, replica_groups=mesh['section'=32,'tensor'=16] {'tensor'}, dimensions={1}, use_global_device_ids=true | all-gather | bytes 557056 | tf_op jit(solution)/shard_map/while/body/eval_jaxpr/all_gather | solution.py:74
  419.7 6.3 collective-permute-start
  427.1 414.6 %while.53 = (s32[]{:T(128)}, bf16[64,256]{1,0:T(8,128)(2,1)S(1)}, bf16[64,256]{1,0:T(8,128)(2,1)S(1)}, f32[256,64]{0,1:T(8,128)}, f32[64,256]{1,0:T(8,128)}, /*i...) while((s32[]{:T(128)}, bf16[64,256]{1,0:T(8,128)(2,1)S(1)}, ...), condition=%wide.region_9.10_spmd.clone, body=%wide.region_4.9_spmd.clone.sunk | while | flops 286040064 | bytes 30409348 | solution.py:146
  427.1 2.3 fusion.128
  429.4 1.1 copy.27
  430.5 4.5 all-to-all-start.1
  435.8 1.1 copy.26
  436.9 14.0 %all-to-all-done.1 = f32[64,16,256]{2,0,1:T(8,128)S(1)} async-done(((f32[64,16,256]{2,0,1:T(8,128)}), f32[64,16,256]{2,0,1:T(8,128)S(1)}, u32[]{:S(2)}, u32[]{:S(2)}) %all-to-all-start.1) | async-done | bytes 1048608 | tf_op jit(solution)/shard_map/while/body/eval_jaxpr/all_to_all | solution.py:126
  450.9 4.3 all-to-all-start
  455.5 58.3 %all-reduce.5 = (bf16[64,64]{1,0:T(8,128)(2,1)S(1)}, bf16[64,64]{1,0:T(8,128)(2,1)S(1)}) all-reduce(f32[64,64]{1,0:T(8,128)S(1)} %fusion.125, f32[64,64]{1,0:T(8,128)S(1)} %fusion.126), channel_id=1, replica_groups=mesh['section'=32,'tensor'=16] {'tensor'}, use_global_device_ids=true, to_apply=%region_6.6 | all-reduce | flops 8192 | bytes 49152 | tf_op jit(solution)/shard_map/while/body/eval_jaxpr/psum | solution.py:113
  514.6 5.9 collective-permute-start.3
  520.8 1.3 collective-permute-start.2
  522.3 5.8 collective-permute-done.2
  528.1 2.3 fusion.128
  530.5 1.1 copy.27
  531.6 9.0 %all-to-all-start.1 = ((f32[64,16,256]{2,0,1:T(8,128)}), f32[64,16,256]{2,0,1:T(8,128)S(1)}, u32[]{:S(2)}, u32[]{:S(2)}) async-start(f32[64,16,256]{2,0,1:T(8,128)} %bitcast.142), calls=%async_computation.1 | async-start | bytes 2097152 | tf_op jit(solution)/shard_map/while/body/eval_jaxpr/all_to_all | solution.py:126
  542.5 14.0 %all-to-all-done.1 = f32[64,16,256]{2,0,1:T(8,128)S(1)} async-done(((f32[64,16,256]{2,0,1:T(8,128)}), f32[64,16,256]{2,0,1:T(8,128)S(1)}, u32[]{:S(2)}, u32[]{:S(2)}) %all-to-all-start.1) | async-done | bytes 1048608 | tf_op jit(solution)/shard_map/while/body/eval_jaxpr/all_to_all | solution.py:126
  556.5 4.3 all-to-all-start
  561.1 58.3 %all-reduce.5 = (bf16[64,64]{1,0:T(8,128)(2,1)S(1)}, bf16[64,64]{1,0:T(8,128)(2,1)S(1)}) all-reduce(f32[64,64]{1,0:T(8,128)S(1)} %fusion.125, f32[64,64]{1,0:T(8,128)S(1)} %fusion.126), channel_id=1, replica_groups=mesh['section'=32,'tensor'=16] {'tensor'}, use_global_device_ids=true, to_apply=%region_6.6 | all-reduce | flops 8192 | bytes 49152 | tf_op jit(solution)/shard_map/while/body/eval_jaxpr/psum | solution.py:113
  620.2 5.7 collective-permute-start.3
  626.2 1.3 collective-permute-start.2
  627.7 5.5 collective-permute-done.2
  633.2 2.3 fusion.128
  635.6 1.1 copy.27
  636.7 9.0 %all-to-all-start.1 = ((f32[64,16,256]{2,0,1:T(8,128)}), f32[64,16,256]{2,0,1:T(8,128)S(1)}, u32[]{:S(2)}, u32[]{:S(2)}) async-start(f32[64,16,256]{2,0,1:T(8,128)} %bitcast.142), calls=%async_computation.1 | async-start | bytes 2097152 | tf_op jit(solution)/shard_map/while/body/eval_jaxpr/all_to_all | solution.py:126
  647.5 14.0 %all-to-all-done.1 = f32[64,16,256]{2,0,1:T(8,128)S(1)} async-done(((f32[64,16,256]{2,0,1:T(8,128)}), f32[64,16,256]{2,0,1:T(8,128)S(1)}, u32[]{:S(2)}, u32[]{:S(2)}) %all-to-all-start.1) | async-done | bytes 1048608 | tf_op jit(solution)/shard_map/while/body/eval_jaxpr/all_to_all | solution.py:126
  661.6 4.3 all-to-all-start
  666.1 58.3 %all-reduce.5 = (bf16[64,64]{1,0:T(8,128)(2,1)S(1)}, bf16[64,64]{1,0:T(8,128)(2,1)S(1)}) all-reduce(f32[64,64]{1,0:T(8,128)S(1)} %fusion.125, f32[64,64]{1,0:T(8,128)S(1)} %fusion.126), channel_id=1, replica_groups=mesh['section'=32,'tensor'=16] {'tensor'}, use_global_device_ids=true, to_apply=%region_6.6 | all-reduce | flops 8192 | bytes 49152 | tf_op jit(solution)/shard_map/while/body/eval_jaxpr/psum | solution.py:113
  725.3 6.6 collective-permute-start.3
  732.2 1.3 collective-permute-start.2
  733.7 4.3 collective-permute-done.2
  738.0 2.3 fusion.128
  740.4 1.1 copy.27
  741.5 9.0 %all-to-all-start.1 = ((f32[64,16,256]{2,0,1:T(8,128)}), f32[64,16,256]{2,0,1:T(8,128)S(1)}, u32[]{:S(2)}, u32[]{:S(2)}) async-start(f32[64,16,256]{2,0,1:T(8,128)} %bitcast.142), calls=%async_computation.1 | async-start | bytes 2097152 | tf_op jit(solution)/shard_map/while/body/eval_jaxpr/all_to_all | solution.py:126
  751.3 1.1 copy.26
  752.3 14.0 %all-to-all-done.1 = f32[64,16,256]{2,0,1:T(8,128)S(1)} async-done(((f32[64,16,256]{2,0,1:T(8,128)}), f32[64,16,256]{2,0,1:T(8,128)S(1)}, u32[]{:S(2)}, u32[]{:S(2)}) %all-to-all-start.1) | async-done | bytes 1048608 | tf_op jit(solution)/shard_map/while/body/eval_jaxpr/all_to_all | solution.py:126
  766.4 4.3 all-to-all-start
  770.9 58.3 %all-reduce.5 = (bf16[64,64]{1,0:T(8,128)(2,1)S(1)}, bf16[64,64]{1,0:T(8,128)(2,1)S(1)}) all-reduce(f32[64,64]{1,0:T(8,128)S(1)} %fusion.125, f32[64,64]{1,0:T(8,128)S(1)} %fusion.126), channel_id=1, replica_groups=mesh['section'=32,'tensor'=16] {'tensor'}, use_global_device_ids=true, to_apply=%region_6.6 | all-reduce | flops 8192 | bytes 49152 | tf_op jit(solution)/shard_map/while/body/eval_jaxpr/psum | solution.py:113
  830.1 5.7 collective-permute-start.3
  836.1 1.3 collective-permute-start.2
  837.6 4.0 collective-permute-done.2
  (215 shorter events, 22.3 us)
Async XLA Ops:
  3.3 78.1 %copy-start.4 = (bf16[64,256]{1,0:T(8,128)(2,1)S(1)}, bf16[64,256]{1,0:T(8,128)(2,1)}, u32[]{:S(2)}) copy-start(bf16[64,256]{1,0:T(8,128)(2,1)} %get-tuple-element.1042) | copy-start | bytes 98308 | tf_op jit(solution)/shard_map/while
  3.3 102.7 %copy-start = (bf16[4096,256]{1,0:T(8,128)(2,1)S(1)}, bf16[4096,256]{1,0:T(8,128)(2,1)}, u32[]{:S(2)}) copy-start(bf16[4096,256]{1,0:T(8,128)(2,1)} %get-tuple-element.1037) | copy-start | bytes 6291460 | tf_op jit(solution)/shard_map/while
  81.4 25.1 %copy-start.2 = (bf16[64,256]{1,0:T(8,128)(2,1)S(1)}, bf16[64,256]{1,0:T(8,128)(2,1)}, u32[]{:S(2)}) copy-start(bf16[64,256]{1,0:T(8,128)(2,1)} %get-tuple-element.1039) | copy-start | bytes 98308 | tf_op jit(solution)/shard_map/while
  81.5 30.4 %collective-permute-start.1 = (bf16[64,256]{1,0:T(8,128)(2,1)S(1)}, bf16[64,256]{1,0:T(8,128)(2,1)S(1)}, u32[]{:S(2)}, u32[]{:S(2)}) collective-permute-start(bf16[64,256]{1,0:T(8,128)(2,1)S(1)} %get-tuple-element.963), channel_id=1, source_target_pairs={{16,0},{32,16},{48,32},{64,48},{80,64},{96,80},{112,96},{128,112},... | collective-permute-start | bytes 98312 | tf_op jit(solution)/shard_map/while/body/eval_jaxpr/ppermute | solution.py:15
  106.6 6.2 collective-permute-start
  112.8 72.4 %copy-start.4 = (bf16[64,256]{1,0:T(8,128)(2,1)S(1)}, bf16[64,256]{1,0:T(8,128)(2,1)}, u32[]{:S(2)}) copy-start(bf16[64,256]{1,0:T(8,128)(2,1)} %get-tuple-element.1042) | copy-start | bytes 98308 | tf_op jit(solution)/shard_map/while
  112.8 97.0 %copy-start = (bf16[4096,256]{1,0:T(8,128)(2,1)S(1)}, bf16[4096,256]{1,0:T(8,128)(2,1)}, u32[]{:S(2)}) copy-start(bf16[4096,256]{1,0:T(8,128)(2,1)} %get-tuple-element.1037) | copy-start | bytes 6291460 | tf_op jit(solution)/shard_map/while
  185.2 25.1 %copy-start.2 = (bf16[64,256]{1,0:T(8,128)(2,1)S(1)}, bf16[64,256]{1,0:T(8,128)(2,1)}, u32[]{:S(2)}) copy-start(bf16[64,256]{1,0:T(8,128)(2,1)} %get-tuple-element.1039) | copy-start | bytes 98308 | tf_op jit(solution)/shard_map/while
  185.4 30.5 %collective-permute-start.1 = (bf16[64,256]{1,0:T(8,128)(2,1)S(1)}, bf16[64,256]{1,0:T(8,128)(2,1)S(1)}, u32[]{:S(2)}, u32[]{:S(2)}) collective-permute-start(bf16[64,256]{1,0:T(8,128)(2,1)S(1)} %get-tuple-element.963), channel_id=1, source_target_pairs={{16,0},{32,16},{48,32},{64,48},{80,64},{96,80},{112,96},{128,112},... | collective-permute-start | bytes 98312 | tf_op jit(solution)/shard_map/while/body/eval_jaxpr/ppermute | solution.py:15
  210.5 6.3 collective-permute-start
  216.8 72.3 %copy-start.4 = (bf16[64,256]{1,0:T(8,128)(2,1)S(1)}, bf16[64,256]{1,0:T(8,128)(2,1)}, u32[]{:S(2)}) copy-start(bf16[64,256]{1,0:T(8,128)(2,1)} %get-tuple-element.1042) | copy-start | bytes 98308 | tf_op jit(solution)/shard_map/while
  216.8 96.9 %copy-start = (bf16[4096,256]{1,0:T(8,128)(2,1)S(1)}, bf16[4096,256]{1,0:T(8,128)(2,1)}, u32[]{:S(2)}) copy-start(bf16[4096,256]{1,0:T(8,128)(2,1)} %get-tuple-element.1037) | copy-start | bytes 6291460 | tf_op jit(solution)/shard_map/while
  289.1 25.1 %copy-start.2 = (bf16[64,256]{1,0:T(8,128)(2,1)S(1)}, bf16[64,256]{1,0:T(8,128)(2,1)}, u32[]{:S(2)}) copy-start(bf16[64,256]{1,0:T(8,128)(2,1)} %get-tuple-element.1039) | copy-start | bytes 98308 | tf_op jit(solution)/shard_map/while
  289.2 31.7 %collective-permute-start.1 = (bf16[64,256]{1,0:T(8,128)(2,1)S(1)}, bf16[64,256]{1,0:T(8,128)(2,1)S(1)}, u32[]{:S(2)}, u32[]{:S(2)}) collective-permute-start(bf16[64,256]{1,0:T(8,128)(2,1)S(1)} %get-tuple-element.963), channel_id=1, source_target_pairs={{16,0},{32,16},{48,32},{64,48},{80,64},{96,80},{112,96},{128,112},... | collective-permute-start | bytes 98312 | tf_op jit(solution)/shard_map/while/body/eval_jaxpr/ppermute | solution.py:15
  314.4 7.5 collective-permute-start
  321.9 72.6 %copy-start.4 = (bf16[64,256]{1,0:T(8,128)(2,1)S(1)}, bf16[64,256]{1,0:T(8,128)(2,1)}, u32[]{:S(2)}) copy-start(bf16[64,256]{1,0:T(8,128)(2,1)} %get-tuple-element.1042) | copy-start | bytes 98308 | tf_op jit(solution)/shard_map/while
  321.9 97.2 %copy-start = (bf16[4096,256]{1,0:T(8,128)(2,1)S(1)}, bf16[4096,256]{1,0:T(8,128)(2,1)}, u32[]{:S(2)}) copy-start(bf16[4096,256]{1,0:T(8,128)(2,1)} %get-tuple-element.1037) | copy-start | bytes 6291460 | tf_op jit(solution)/shard_map/while
  394.4 25.1 %copy-start.2 = (bf16[64,256]{1,0:T(8,128)(2,1)S(1)}, bf16[64,256]{1,0:T(8,128)(2,1)}, u32[]{:S(2)}) copy-start(bf16[64,256]{1,0:T(8,128)(2,1)} %get-tuple-element.1039) | copy-start | bytes 98308 | tf_op jit(solution)/shard_map/while
  394.6 31.5 %collective-permute-start.1 = (bf16[64,256]{1,0:T(8,128)(2,1)S(1)}, bf16[64,256]{1,0:T(8,128)(2,1)S(1)}, u32[]{:S(2)}, u32[]{:S(2)}) collective-permute-start(bf16[64,256]{1,0:T(8,128)(2,1)S(1)} %get-tuple-element.963), channel_id=1, source_target_pairs={{16,0},{32,16},{48,32},{64,48},{80,64},{96,80},{112,96},{128,112},... | collective-permute-start | bytes 98312 | tf_op jit(solution)/shard_map/while/body/eval_jaxpr/ppermute | solution.py:15
  419.7 7.4 collective-permute-start
  430.5 20.4 %all-to-all-start.1 = ((f32[64,16,256]{2,0,1:T(8,128)}), f32[64,16,256]{2,0,1:T(8,128)S(1)}, u32[]{:S(2)}, u32[]{:S(2)}) async-start(f32[64,16,256]{2,0,1:T(8,128)} %bitcast.142), calls=%async_computation.1 | async-start | bytes 2097152 | tf_op jit(solution)/shard_map/while/body/eval_jaxpr/all_to_all | solution.py:126
  435.8 19.5 %copy-start.5 = (bf16[64,256]{1,0:T(8,128)(2,1)S(1)}, bf16[64,256]{1,0:T(8,128)(2,1)}, u32[]{:S(2)}) copy-start(bf16[64,256]{1,0:T(8,128)(2,1)} %get-tuple-element.1102) | copy-start | bytes 98308 | tf_op jit(solution)/shard_map/while
  435.8 19.6 %copy-start.3 = (bf16[64,256]{1,0:T(8,128)(2,1)S(1)}, bf16[64,256]{1,0:T(8,128)(2,1)}, u32[]{:S(2)}) copy-start(bf16[64,256]{1,0:T(8,128)(2,1)} %get-tuple-element.1099) | copy-start | bytes 98308 | tf_op jit(solution)/shard_map/while
  435.8 78.0 %copy-start.8 = (f32[64,256]{1,0:T(8,128)S(1)}, f32[64,256]{1,0:T(8,128)}, u32[]{:S(2)}) copy-start(f32[64,256]{1,0:T(8,128)} %get-tuple-element.1073) | copy-start | bytes 196612 | tf_op jit(solution)/shard_map/while
  435.8 78.0 %copy-start.13 = (bf16[64,64]{1,0:T(8,128)(2,1)S(1)}, bf16[64,64]{1,0:T(8,128)(2,1)}, u32[]{:S(2)}) copy-start(bf16[64,64]{1,0:T(8,128)(2,1)} %copy-done.12) | copy-start | bytes 24580 | tf_op jit(solution)/shard_map/while
  435.8 78.2 %copy-start.10 = (f32[256,64]{0,1:T(8,128)S(1)}, f32[256,64]{0,1:T(8,128)}, u32[]{:S(2)}) copy-start(f32[256,64]{0,1:T(8,128)} %get-tuple-element.1072) | copy-start | bytes 196612 | tf_op jit(solution)/shard_map/while
  450.9 69.6 %all-to-all-start = ((f32[64,16,256]{2,0,1:T(8,128)}), f32[64,16,256]{2,0,1:T(8,128)S(1)}, u32[]{:S(2)}, u32[]{:S(2)}) async-start(f32[64,16,256]{2,0,1:T(8,128)} %bitcast.135), calls=%async_computation | async-start | bytes 2097152 | tf_op jit(solution)/shard_map/while/body/eval_jaxpr/all_to_all | solution.py:125
  514.0 14.2 %copy-start.9 = (f32[64,256]{1,0:T(8,128)}, f32[64,256]{1,0:T(8,128)S(1)}, u32[]{:S(2)}) copy-start(f32[64,256]{1,0:T(8,128)S(1)} %convolution_select_fusion.4) | copy-start | bytes 196612 | tf_op jit(solution)/shard_map/while
  514.2 13.9 %copy-start.11 = (f32[256,64]{0,1:T(8,128)}, f32[256,64]{0,1:T(8,128)S(1)}, u32[]{:S(2)}) copy-start(f32[256,64]{0,1:T(8,128)S(1)} %fusion.130) | copy-start | bytes 196612 | tf_op jit(solution)/shard_map/while
  514.6 7.6 collective-permute-start.3
  520.8 7.4 collective-permute-start.2
  531.6 24.9 %all-to-all-start.1 = ((f32[64,16,256]{2,0,1:T(8,128)}), f32[64,16,256]{2,0,1:T(8,128)S(1)}, u32[]{:S(2)}, u32[]{:S(2)}) async-start(f32[64,16,256]{2,0,1:T(8,128)} %bitcast.142), calls=%async_computation.1 | async-start | bytes 2097152 | tf_op jit(solution)/shard_map/while/body/eval_jaxpr/all_to_all | solution.py:126
  541.3 19.5 %copy-start.5 = (bf16[64,256]{1,0:T(8,128)(2,1)S(1)}, bf16[64,256]{1,0:T(8,128)(2,1)}, u32[]{:S(2)}) copy-start(bf16[64,256]{1,0:T(8,128)(2,1)} %get-tuple-element.1102) | copy-start | bytes 98308 | tf_op jit(solution)/shard_map/while
  541.3 19.6 %copy-start.3 = (bf16[64,256]{1,0:T(8,128)(2,1)S(1)}, bf16[64,256]{1,0:T(8,128)(2,1)}, u32[]{:S(2)}) copy-start(bf16[64,256]{1,0:T(8,128)(2,1)} %get-tuple-element.1099) | copy-start | bytes 98308 | tf_op jit(solution)/shard_map/while
  541.3 78.0 %copy-start.8 = (f32[64,256]{1,0:T(8,128)S(1)}, f32[64,256]{1,0:T(8,128)}, u32[]{:S(2)}) copy-start(f32[64,256]{1,0:T(8,128)} %get-tuple-element.1073) | copy-start | bytes 196612 | tf_op jit(solution)/shard_map/while
  541.4 78.0 %copy-start.13 = (bf16[64,64]{1,0:T(8,128)(2,1)S(1)}, bf16[64,64]{1,0:T(8,128)(2,1)}, u32[]{:S(2)}) copy-start(bf16[64,64]{1,0:T(8,128)(2,1)} %copy-done.12) | copy-start | bytes 24580 | tf_op jit(solution)/shard_map/while
  541.4 78.2 %copy-start.10 = (f32[256,64]{0,1:T(8,128)S(1)}, f32[256,64]{0,1:T(8,128)}, u32[]{:S(2)}) copy-start(f32[256,64]{0,1:T(8,128)} %get-tuple-element.1072) | copy-start | bytes 196612 | tf_op jit(solution)/shard_map/while
  556.5 69.5 %all-to-all-start = ((f32[64,16,256]{2,0,1:T(8,128)}), f32[64,16,256]{2,0,1:T(8,128)S(1)}, u32[]{:S(2)}, u32[]{:S(2)}) async-start(f32[64,16,256]{2,0,1:T(8,128)} %bitcast.135), calls=%async_computation | async-start | bytes 2097152 | tf_op jit(solution)/shard_map/while/body/eval_jaxpr/all_to_all | solution.py:125
  619.5 13.7 %copy-start.9 = (f32[64,256]{1,0:T(8,128)}, f32[64,256]{1,0:T(8,128)S(1)}, u32[]{:S(2)}) copy-start(f32[64,256]{1,0:T(8,128)S(1)} %convolution_select_fusion.4) | copy-start | bytes 196612 | tf_op jit(solution)/shard_map/while
  619.7 13.4 %copy-start.11 = (f32[256,64]{0,1:T(8,128)}, f32[256,64]{0,1:T(8,128)S(1)}, u32[]{:S(2)}) copy-start(f32[256,64]{0,1:T(8,128)S(1)} %fusion.130) | copy-start | bytes 196612 | tf_op jit(solution)/shard_map/while
  620.2 7.5 collective-permute-start.3
  626.2 7.0 collective-permute-start.2
  636.7 24.9 %all-to-all-start.1 = ((f32[64,16,256]{2,0,1:T(8,128)}), f32[64,16,256]{2,0,1:T(8,128)S(1)}, u32[]{:S(2)}, u32[]{:S(2)}) async-start(f32[64,16,256]{2,0,1:T(8,128)} %bitcast.142), calls=%async_computation.1 | async-start | bytes 2097152 | tf_op jit(solution)/shard_map/while/body/eval_jaxpr/all_to_all | solution.py:126
  646.4 19.5 %copy-start.5 = (bf16[64,256]{1,0:T(8,128)(2,1)S(1)}, bf16[64,256]{1,0:T(8,128)(2,1)}, u32[]{:S(2)}) copy-start(bf16[64,256]{1,0:T(8,128)(2,1)} %get-tuple-element.1102) | copy-start | bytes 98308 | tf_op jit(solution)/shard_map/while
  646.4 19.6 %copy-start.3 = (bf16[64,256]{1,0:T(8,128)(2,1)S(1)}, bf16[64,256]{1,0:T(8,128)(2,1)}, u32[]{:S(2)}) copy-start(bf16[64,256]{1,0:T(8,128)(2,1)} %get-tuple-element.1099) | copy-start | bytes 98308 | tf_op jit(solution)/shard_map/while
  646.4 78.0 %copy-start.8 = (f32[64,256]{1,0:T(8,128)S(1)}, f32[64,256]{1,0:T(8,128)}, u32[]{:S(2)}) copy-start(f32[64,256]{1,0:T(8,128)} %get-tuple-element.1073) | copy-start | bytes 196612 | tf_op jit(solution)/shard_map/while
  646.4 78.0 %copy-start.13 = (bf16[64,64]{1,0:T(8,128)(2,1)S(1)}, bf16[64,64]{1,0:T(8,128)(2,1)}, u32[]{:S(2)}) copy-start(bf16[64,64]{1,0:T(8,128)(2,1)} %copy-done.12) | copy-start | bytes 24580 | tf_op jit(solution)/shard_map/while
  646.4 78.2 %copy-start.10 = (f32[256,64]{0,1:T(8,128)S(1)}, f32[256,64]{0,1:T(8,128)}, u32[]{:S(2)}) copy-start(f32[256,64]{0,1:T(8,128)} %get-tuple-element.1072) | copy-start | bytes 196612 | tf_op jit(solution)/shard_map/while
  661.6 70.4 %all-to-all-start = ((f32[64,16,256]{2,0,1:T(8,128)}), f32[64,16,256]{2,0,1:T(8,128)S(1)}, u32[]{:S(2)}, u32[]{:S(2)}) async-start(f32[64,16,256]{2,0,1:T(8,128)} %bitcast.135), calls=%async_computation | async-start | bytes 2097152 | tf_op jit(solution)/shard_map/while/body/eval_jaxpr/all_to_all | solution.py:125
  724.6 13.4 %copy-start.9 = (f32[64,256]{1,0:T(8,128)}, f32[64,256]{1,0:T(8,128)S(1)}, u32[]{:S(2)}) copy-start(f32[64,256]{1,0:T(8,128)S(1)} %convolution_select_fusion.4) | copy-start | bytes 196612 | tf_op jit(solution)/shard_map/while
  724.8 13.2 %copy-start.11 = (f32[256,64]{0,1:T(8,128)}, f32[256,64]{0,1:T(8,128)S(1)}, u32[]{:S(2)}) copy-start(f32[256,64]{0,1:T(8,128)S(1)} %fusion.130) | copy-start | bytes 196612 | tf_op jit(solution)/shard_map/while
  725.3 8.4 collective-permute-start.3
  732.2 5.8 collective-permute-start.2
  741.5 24.9 %all-to-all-start.1 = ((f32[64,16,256]{2,0,1:T(8,128)}), f32[64,16,256]{2,0,1:T(8,128)S(1)}, u32[]{:S(2)}, u32[]{:S(2)}) async-start(f32[64,16,256]{2,0,1:T(8,128)} %bitcast.142), calls=%async_computation.1 | async-start | bytes 2097152 | tf_op jit(solution)/shard_map/while/body/eval_jaxpr/all_to_all | solution.py:126
  751.2 19.5 %copy-start.5 = (bf16[64,256]{1,0:T(8,128)(2,1)S(1)}, bf16[64,256]{1,0:T(8,128)(2,1)}, u32[]{:S(2)}) copy-start(bf16[64,256]{1,0:T(8,128)(2,1)} %get-tuple-element.1102) | copy-start | bytes 98308 | tf_op jit(solution)/shard_map/while
  751.2 19.6 %copy-start.3 = (bf16[64,256]{1,0:T(8,128)(2,1)S(1)}, bf16[64,256]{1,0:T(8,128)(2,1)}, u32[]{:S(2)}) copy-start(bf16[64,256]{1,0:T(8,128)(2,1)} %get-tuple-element.1099) | copy-start | bytes 98308 | tf_op jit(solution)/shard_map/while
  751.2 78.0 %copy-start.8 = (f32[64,256]{1,0:T(8,128)S(1)}, f32[64,256]{1,0:T(8,128)}, u32[]{:S(2)}) copy-start(f32[64,256]{1,0:T(8,128)} %get-tuple-element.1073) | copy-start | bytes 196612 | tf_op jit(solution)/shard_map/while
  751.2 78.0 %copy-start.13 = (bf16[64,64]{1,0:T(8,128)(2,1)S(1)}, bf16[64,64]{1,0:T(8,128)(2,1)}, u32[]{:S(2)}) copy-start(bf16[64,64]{1,0:T(8,128)(2,1)} %copy-done.12) | copy-start | bytes 24580 | tf_op jit(solution)/shard_map/while
  751.2 78.2 %copy-start.10 = (f32[256,64]{0,1:T(8,128)S(1)}, f32[256,64]{0,1:T(8,128)}, u32[]{:S(2)}) copy-start(f32[256,64]{0,1:T(8,128)} %get-tuple-element.1072) | copy-start | bytes 196612 | tf_op jit(solution)/shard_map/while
  766.4 69.5 %all-to-all-start = ((f32[64,16,256]{2,0,1:T(8,128)}), f32[64,16,256]{2,0,1:T(8,128)S(1)}, u32[]{:S(2)}, u32[]{:S(2)}) async-start(f32[64,16,256]{2,0,1:T(8,128)} %bitcast.135), calls=%async_computation | async-start | bytes 2097152 | tf_op jit(solution)/shard_map/while/body/eval_jaxpr/all_to_all | solution.py:125
  829.4 12.2 %copy-start.9 = (f32[64,256]{1,0:T(8,128)}, f32[64,256]{1,0:T(8,128)S(1)}, u32[]{:S(2)}) copy-start(f32[64,256]{1,0:T(8,128)S(1)} %convolution_select_fusion.4) | copy-start | bytes 196612 | tf_op jit(solution)/shard_map/while
  829.6 12.0 %copy-start.11 = (f32[256,64]{0,1:T(8,128)}, f32[256,64]{0,1:T(8,128)S(1)}, u32[]{:S(2)}) copy-start(f32[256,64]{0,1:T(8,128)S(1)} %fusion.130) | copy-start | bytes 196612 | tf_op jit(solution)/shard_map/while
  830.1 7.5 collective-permute-start.3
  836.1 5.6 collective-permute-start.2
  (10 other events, 46.5 us)
where the time goes:
time: 855 us; the launch traced here: 842 us
  blocking collectives  612 us (72%)
  starting transfers between devices  106 us (12%)
  waiting for transfers between devices  79.5 us (9%)
  matrix products  29.7 us (3%)
  local copies, waits for them, and re-layouts  12.2 us (1%)
    psum x4, blocking collectives, backward_step(): lax.psum((jnp.dot(e_down, down_adapter_upper.T, preferred_element_type=jn...  233 us
    psum x4, blocking collectives, forward_step(): lax.psum((partial_coeff(buf_down, down_adapter_lower), partial_coeff(buf_...  198 us
    all_gather x4, blocking collectives, forward_step(): lax.all_gather(buf_down, 'tensor', axis=1, tiled=True)  92.8 us
    all_gather x4, blocking collectives, forward_step(): lax.all_gather(buf_up, 'tensor', axis=1, tiled=True)  88 us
    ppermute x16, starting transfers between devices, from_behind(): lax.ppermute(value, axis, [(source, source + steps) for source in range(l...  57.7 us
    all_to_all x4, waiting for transfers between devices, backward_step(): lax.all_to_all(terms_up, 'tensor', split_axis=1, concat_axis=0, tiled=True)  56.1 us
    all_to_all x4, starting transfers between devices, backward_step(): lax.all_to_all(terms_up, 'tensor', split_axis=1, concat_axis=0, tiled=True)  31.4 us
    ppermute x16, waiting for transfers between devices, from_behind(): lax.ppermute(value, axis, [(source, source + steps) for source in range(l...  23.4 us
  transfers between devices with their start and end apart: 24, of which 12 were waited for; matrix products, arithmetic and copies ran while one was open for 2% of the time, Pallas kernels for 0%

commit v1 on v0

v1 whole, which is shorter than its diff:
```python
import functools

import jax
import jax.numpy as jnp
from jax import lax
from jax.experimental import pallas as pl
from jax.experimental.pallas import tpu as pltpu
from jax.sharding import PartitionSpec as P

MESH = pl.DeviceIdType.MESH
F32, BF16 = jnp.float32, jnp.bfloat16
LAYERS = 4
CHIPS = 8
TOK = 64
COLS = 256
RANK = 64
SPLIT = 2
ROWS = TOK // SPLIT
SCALE = 2.0
FAR = (5, 4, 7, 3, 6, 2, 1)
NEAR = (0, 1, 2, 6, 3, 7, 4, 5)


def nn(a, b):
    return jnp.dot(a, b, preferred_element_type=F32)


def nt(a, b):
    return lax.dot_general(a, b, (((1,), (1,)), ((), ())), preferred_element_type=F32)


def tn(a, b):
    return lax.dot_general(a, b, (((0,), (0,)), ((), ())), preferred_element_type=F32)


def fold(v):
    return jnp.concatenate([v[: TOK // 2], v[TOK // 2 :]], axis=1)


def unfold(v):
    return jnp.concatenate([v[:, :RANK], v[:, RANK:]], axis=0)


def kernel(
    xd, xu, atd, atu, bd, bu, wd, wu,
    gad, gbd, gau, gbu,
    w, weff, at, bch, hb, xs, xp, hout, eb, ps, pr, eout, gs, gr, cs, cr,
    ld_x, ld_a, ld_b, ld_w,
    w_s, w_r, b_s, b_r, a_s, a_r, h_s, h_r, hx_s, hx_r, hc_s, hc_r,
    ec_s, ec_r, ex_s, ex_r, p_s, p_r, g_s, g_r, c_s, c_r,
):
    sec, t = lax.axis_index("section"), lax.axis_index("tensor")
    group, s = sec // LAYERS, sec % LAYERS
    chip, core = t // 2, t % 2
    low = s < 2
    q1 = jnp.where(low, s, LAYERS - 1 - s)
    toward = jnp.where(low, 1, -1)
    sibling = (sec, t ^ 1)

    def peer(m):
        return (sec, t ^ (2 * m))

    def rows(i):
        return pl.ds(i * ROWS, ROWS)

    def remote(src, dst, send, recv, to):
        return pltpu.make_async_remote_copy(
            src_ref=src, dst_ref=dst, send_sem=send, recv_sem=recv,
            device_id=to, device_id_type=MESH,
        )

    def start_local(r, down):
        x, a, b, v = (xd, atd, bd, wd) if down else (xu, atu, bu, wu)
        if r == 0:

            @pl.when(q1 == 0)
            def _():
                pltpu.make_async_copy(x.at[group], hb.at[0, 0], ld_x).start()

        pltpu.make_async_copy(a, at.at[r, 0], ld_a.at[r]).start()
        pltpu.make_async_copy(b, bch.at[r, 0], ld_b.at[r]).start()
        pltpu.make_async_copy(v.at[:, core], w.at[r, 0], ld_w.at[r]).start()

    @pl.when(low)
    def _():
        start_local(0, True)
        start_local(1, False)

    @pl.when(jnp.logical_not(low))
    def _():
        start_local(0, False)
        start_local(1, True)

    barrier = pltpu.get_barrier_semaphore()
    for m in range(1, CHIPS):
        pl.semaphore_signal(barrier, inc=1, device_id=peer(m), device_id_type=MESH)
    pl.semaphore_signal(barrier, inc=1, device_id=sibling, device_id_type=MESH)

    @pl.when(s > 0)
    def _():
        pl.semaphore_signal(barrier, inc=1, device_id=(sec - 1, t), device_id_type=MESH)

    @pl.when(s < LAYERS - 1)
    def _():
        pl.semaphore_signal(barrier, inc=1, device_id=(sec + 1, t), device_id_type=MESH)

    pl.semaphore_wait(barrier, jnp.where(q1 == 0, CHIPS + 1, CHIPS + 2))

    def h_copy(r, i, m):
        return remote(
            hb.at[r, 0, rows(i)], hb.at[r, m, rows(i)], h_s.at[r, i, m], h_r.at[r, i, m], peer(m)
        )

    def a_copy(r, m):
        return remote(at.at[r, 0], at.at[r, m], a_s.at[r, m], a_r.at[r, m], peer(m))

    def b_copy(r):
        return remote(bch.at[r, 0], bch.at[r, 1], b_s.at[r], b_r.at[r], sibling)

    def w_copy(r, down):
        v = wd if down else wu
        return remote(v.at[:, 1 - core], w.at[r, 1], w_s.at[r], w_r.at[r], sibling)

    @pl.when(q1 == 0)
    def _():
        pltpu.make_async_copy(xd.at[group], hb.at[0, 0], ld_x).wait()
        for i in range(SPLIT):
            for m in FAR:
                h_copy(0, i, m).start()

    def share_weights(r):
        pltpu.make_async_copy(atd, at.at[r, 0], ld_a.at[r]).wait()
        for m in FAR:
            a_copy(r, m).start()

        @pl.when(low == (r == 0))
        def _():
            w_copy(r, True).start()

        @pl.when(low != (r == 0))
        def _():
            w_copy(r, False).start()

        pltpu.make_async_copy(bd, bch.at[r, 0], ld_b.at[r]).wait()
        b_copy(r).start()

    share_weights(0)
    share_weights(1)

    def combine_weights(r):
        b_copy(r).wait_recv()
        pltpu.make_async_copy(wd.at[:, core], w.at[r, 0], ld_w.at[r]).wait()
        w_copy(r, True).wait_recv()
        for m in NEAR:
            if m:
                a_copy(r, m).wait_recv()
            j = chip ^ m
            for half in range(2):
                low_rank = tn(at[r, m], bch[r, half])
                weff[r, j, :, half * COLS : (half + 1) * COLS] = (
                    w[r, half, j].astype(F32) + SCALE * low_rank
                ).astype(BF16)

    def hx_copy(r, i):
        return remote(xs.at[r, rows(i)], xp.at[r, rows(i)], hx_s.at[r, i], hx_r.at[r, i], sibling)

    def hc_copy(r, i):
        to = (sec + toward, t) if r == 0 else (sec - toward, t)
        there = q1 if r == 0 else 1
        return remote(
            hout.at[r, rows(i)], hb.at[there, 0, rows(i)], hc_s.at[r, i], hc_r.at[there, i], to
        )

    def hc_arrived(r, i):
        remote(
            hout.at[r, rows(i)], hb.at[r, 0, rows(i)], hc_s.at[r, i], hc_r.at[r, i], sibling
        ).wait_recv()

    def gather(r):
        for i in range(SPLIT):
            hc_arrived(r, i)
            for m in FAR:
                h_copy(r, i, m).start()

    def forward(r):
        own = []
        for i in range(SPLIT):
            total = jnp.zeros((ROWS, 2 * COLS), F32)
            for m in NEAR:
                if m:
                    h_copy(r, i, m).wait_recv()
                total = total + nn(hb[r, m, i * ROWS : (i + 1) * ROWS], weff[r, chip ^ m])
            xs[r, i * ROWS : (i + 1) * ROWS] = total[:, COLS:]
            hx_copy(r, i).start()
            own.append(total[:, :COLS])
        for i in range(SPLIT):
            piece = slice(i * ROWS, (i + 1) * ROWS)
            hx_copy(r, i).wait_recv()
            out = (hb[r, 0, piece].astype(F32) + own[i] + xp[r, piece]).astype(BF16)
            if r == 0:
                hout[r, piece] = out
                hc_copy(r, i).start()
            else:

                @pl.when(q1 == 1)
                def _():
                    hout[r, piece] = out
                    hc_copy(r, i).start()

                @pl.when(q1 == 0)
                def _():
                    eb[r, 0, piece] = out

    def c_copy(r):
        return remote(cs.at[r], cr.at[r], c_s.at[r], c_r.at[r], sibling)

    def coefficients(r):
        total = nt(hb[r, 0], at[r, 0])
        for m in range(1, CHIPS):
            total = total + nt(hb[r, m], at[r, m])
        cs[r] = fold(SCALE * total)
        c_copy(r).start()

    def drain_forward(r):
        for i in range(SPLIT):
            for m in FAR:
                h_copy(r, i, m).wait_send()
            hx_copy(r, i).wait_send()
            if r == 0:
                hc_copy(r, i).wait_send()
            else:

                @pl.when(q1 == 1)
                def _():
                    hc_copy(r, i).wait_send()

    def drain_weights(r):
        for m in FAR:
            a_copy(r, m).wait_send()
        b_copy(r).wait_send()
        w_copy(r, True).wait_send()

    combine_weights(0)

    @pl.when(q1 == 1)
    def _():
        gather(0)

    forward(0)
    combine_weights(1)
    coefficients(0)
    drain_weights(0)
    drain_weights(1)
    drain_forward(0)

    gather(1)
    forward(1)

    def ec_copy(r, i):
        to = (sec - toward, t) if r == 0 else (sec + toward, t)
        there = 0 if r == 0 else 1 - q1
        return remote(
            eout.at[r, rows(i)], eb.at[there, 0, rows(i)], ec_s.at[r, i], ec_r.at[there, i], to
        )

    def ec_arrived(r, i):
        remote(
            eout.at[r, rows(i)], eb.at[r, 0, rows(i)], ec_s.at[r, i], ec_r.at[r, i], sibling
        ).wait_recv()

    def ex_copy(r, i):
        return remote(
            eb.at[r, 0, rows(i)], eb.at[r, 1, rows(i)], ex_s.at[r, i], ex_r.at[r, i], sibling
        )

    def p_copy(r, i, m):
        return remote(
            ps.at[r, m, rows(i)], pr.at[r, m, rows(i)], p_s.at[r, i, m], p_r.at[r, i, m], peer(m)
        )

    def g_copy(r, m):
        return remote(gs.at[r], gr.at[r, m], g_s.at[r, m], g_r.at[r, m], peer(m))

    def arrive(r):
        for i in range(SPLIT):
            if r == 0:
                ec_arrived(r, i)
            else:

                @pl.when(q1 == 1)
                def _():
                    ec_arrived(r, i)

            ex_copy(r, i).start()

    def sum_g(r):
        total = nt(eb[r, 0], bch[r, 0]) + nt(eb[r, 1], bch[r, 1])
        gs[r] = fold(total)
        for m in FAR:
            g_copy(r, m).start()

    def backward(r):
        own = []
        for i in range(SPLIT):
            piece = slice(i * ROWS, (i + 1) * ROWS)
            e_own, e_other = eb[r, 0, piece], eb[r, 1, piece]
            for m in FAR + (0,):
                block = weff.at[r, chip ^ m]
                part = nt(e_own, block[:, :COLS]) + nt(e_other, block[:, COLS:])
                if m:
                    ps[r, m, piece] = part.astype(BF16)
                    p_copy(r, i, m).start()
                else:
                    own.append(part)
        for i in range(SPLIT):
            piece = slice(i * ROWS, (i + 1) * ROWS)
            total = eb[r, 0, piece].astype(F32) + own[i]
            for m in NEAR[1:]:
                p_copy(r, i, m).wait_recv()
                total = total + pr[r, m, piece].astype(F32)
            eout[r, piece] = total.astype(BF16)
            ec_copy(r, i).start()

    def drain_backward(r):
        for i in range(SPLIT):
            for m in FAR:
                p_copy(r, i, m).wait_send()
            ec_copy(r, i).wait_send()

    def finish(r):
        c_copy(r).wait_recv()
        c = unfold(cs[r] + cr[r]).astype(BF16)
        grad_b = tn(c, eb[r, 0])
        total = gs[r]
        for m in NEAR[1:]:
            g_copy(r, m).wait_recv()
            total = total + gr[r, m]
        g = unfold(total).astype(BF16)
        grad_a = SCALE * tn(g, hb[r, 0])

        @pl.when(low == (r == 0))
        def _():
            gad[...] = grad_a
            gbd[...] = grad_b

        @pl.when(low != (r == 0))
        def _():
            gau[...] = grad_a
            gbu[...] = grad_b

    def arrived_other(r):
        for i in range(SPLIT):
            ex_copy(r, i).wait_recv()

    arrive(1)
    arrived_other(1)
    backward(1)
    sum_g(1)
    coefficients(1)
    drain_forward(1)
    finish(1)
    drain_backward(1)

    arrive(0)
    arrived_other(0)

    @pl.when(q1 == 1)
    def _():
        backward(0)

    sum_g(0)
    finish(0)

    @pl.when(q1 == 1)
    def _():
        drain_backward(0)

    for r in range(2):
        for i in range(SPLIT):
            ex_copy(r, i).wait_send()
        for m in FAR:
            g_copy(r, m).wait_send()
        c_copy(r).wait_send()


def body(xd, xu, ad, bd, au, bu, wd, wu):
    def chunks(v):
        return v.reshape(CHIPS, 2, COLS, COLS)

    dma = pltpu.SemaphoreType.DMA
    anywhere = pl.BlockSpec(memory_space=pl.ANY)
    vmem = pl.BlockSpec(memory_space=pltpu.VMEM)
    pair = dma((2,))
    halves = dma((2, SPLIT))
    each = dma((2, SPLIT, CHIPS))
    chips = dma((2, CHIPS))
    gad, gbd, gau, gbu = pl.pallas_call(
        kernel,
        out_shape=[jax.ShapeDtypeStruct((RANK, COLS), F32)] * 4,
        in_specs=[anywhere] * 8,
        out_specs=[vmem] * 4,
        scratch_shapes=[
            pltpu.VMEM((2, 2, CHIPS, COLS, COLS), BF16),
            pltpu.VMEM((2, CHIPS, COLS, 2 * COLS), BF16),
            pltpu.VMEM((2, CHIPS, RANK, COLS), BF16),
            pltpu.VMEM((2, 2, RANK, COLS), BF16),
            pltpu.VMEM((2, CHIPS, TOK, COLS), BF16),
            pltpu.VMEM((2, TOK, COLS), F32),
            pltpu.VMEM((2, TOK, COLS), F32),
            pltpu.VMEM((2, TOK, COLS), BF16),
            pltpu.VMEM((2, 2, TOK, COLS), BF16),
            pltpu.VMEM((2, CHIPS, TOK, COLS), BF16),
            pltpu.VMEM((2, CHIPS, TOK, COLS), BF16),
            pltpu.VMEM((2, TOK, COLS), BF16),
            pltpu.VMEM((2, TOK // 2, 2 * RANK), F32),
            pltpu.VMEM((2, CHIPS, TOK // 2, 2 * RANK), F32),
            pltpu.VMEM((2, TOK // 2, 2 * RANK), F32),
            pltpu.VMEM((2, TOK // 2, 2 * RANK), F32),
            dma, pair, pair, pair,
            pair, pair, pair, pair, chips, chips,
            each, each, halves, halves, halves, halves,
            halves, halves, halves, halves,
            each, each, chips, chips, pair, pair,
        ],
        compiler_params=pltpu.CompilerParams(
            collective_id=0, has_side_effects=True, vmem_limit_bytes=40 * 2**20
        ),
        cost_estimate=pl.CostEstimate(
            flops=8 * TOK * LAYERS * 1024 * COLS, bytes_accessed=6 * 2**20, transcendentals=0
        ),
    )(
        xd, xu, ad[0].T, au[0].T, bd[0], bu[0], chunks(wd), chunks(wu)
    )
    return gad.T[None], gbd[None], gau.T[None], gbu[None]


def solution(mesh):
    in_specs = (
        P(None, None, "tensor"),
        P(None, None, "tensor"),
        P("section", "tensor", None),
        P("section", None, "tensor"),
        P("section", "tensor", None),
        P("section", None, "tensor"),
        P("section", None, "tensor"),
        P("section", None, "tensor"),
    )
    out_specs = (
        P("section", "tensor", None),
        P("section", None, "tensor"),
        P("section", "tensor", None),
        P("section", None, "tensor"),
    )
    return jax.shard_map(body, mesh=mesh, in_specs=in_specs, out_specs=out_specs, check_vma=False)
```

time: 855 us -> 99.6 us (0.12); the launches traced: 842 us -> 99.1 us
  blocking collectives: 612 us -> 0 us
  starting transfers between devices: 106 us -> 0 us
  Pallas kernels: 0 us -> 87.8 us
  waiting for transfers between devices: 79.5 us -> 0 us
  matrix products: 29.7 us -> 0 us
    psum x8 -> x0, blocking collectives: 431 us -> none  [the longest x4 233 us: backward_step(): lax.psum((jnp.dot(e_down, down_adapter_upper.T, preferred_element_type=jn...]
    all_gather x8 -> x0, blocking collectives: 181 us -> none  [the longest x4 92.8 us: forward_step(): lax.all_gather(buf_down, 'tensor', axis=1, tiled=True)]
    pallas_call x0 -> x1, Pallas kernels: none -> 87.8 us  [body(): pl.pallas_call(kernel, out_shape=[jax.ShapeDtypeStruct((RANK, COLS), F32)...]
    ppermute x16 -> x0, starting transfers between devices: 57.7 us -> none  [from_behind(): lax.ppermute(value, axis, [(source, source + steps) for source in range(l...]
    all_to_all x8 -> x0, waiting for transfers between devices: 56.1 us -> none  [the longest x4 56.1 us: backward_step(): lax.all_to_all(terms_up, 'tensor', split_axis=1, concat_axis=0, tiled=True)]
    all_to_all x8 -> x0, starting transfers between devices: 48.6 us -> none  [the longest x4 31.4 us: backward_step(): lax.all_to_all(terms_up, 'tensor', split_axis=1, concat_axis=0, tiled=True)]
    dot_general x64 -> x0, matrix products: 29.7 us -> none  [the longest x4 9.37 us: backward_step(): terms_up = jnp.dot(e_up, columns_up.T, preferred_element_type=jnp.float32)]
    ppermute x16 -> x0, waiting for transfers between devices: 23.4 us -> none  [from_behind(): lax.ppermute(value, axis, [(source, source + steps) for source in range(l...]
  transfers between devices with their start and end apart: 24 -> 0, of which waited for: 12 -> 0; matrix products, arithmetic and copies ran while one was open for 2% -> 0% of each run, Pallas kernels for 0% -> 0%
where the time goes in v1:
time: 99.6 us; the launch traced here: 99.1 us
  Pallas kernels  87.8 us (88%)
  local copies, waits for them, and re-layouts  10.6 us (11%)
    pallas_call x1, Pallas kernels, body(): pl.pallas_call(kernel, out_shape=[jax.ShapeDtypeStruct((RANK, COLS), F32)...  87.8 us
    unnamed x20, local copies, waits for them, and re-layouts  10.6 us

profile of v1, /device:TPU:1, one launch (start us, length us, event | category | flops | bytes accessed | tf_op | source)
XLA Modules:
  0.0 99.1 jit_solution(18385817617067331983)
XLA Ops:
  0.6 0.0 copy-start
  0.6 1.6 %copy-done = bf16[1,4096,256]{2,1,0:T(8,128)(2,1)S(1)} copy-done((bf16[1,4096,256]{2,1,0:T(8,128)(2,1)S(1)}, bf16[1,4096,256]{2,1,0:T(8,128)(2,1)}, u32[]{:S(2)}) %copy-start) | copy-done | bytes 2097176
  2.2 0.0 copy-start.1
  2.2 1.6 %copy-done.1 = bf16[1,4096,256]{2,1,0:T(8,128)(2,1)S(1)} copy-done((bf16[1,4096,256]{2,1,0:T(8,128)(2,1)S(1)}, bf16[1,4096,256]{2,1,0:T(8,128)(2,1)}, u32[]{:S(2)}) %copy-start.1) | copy-done | bytes 2097176
  3.8 0.0 copy-start.2
  3.8 0.9 copy-done.2
  4.8 0.0 copy-start.3
  4.8 0.9 copy-done.3
  5.7 0.0 copy-start.4
  5.7 0.8 copy-done.4
  6.5 0.0 copy-start.5
  6.5 0.8 copy-done.5
  7.2 0.0 copy-start.6
  7.2 0.8 copy-done.6
  8.0 0.0 copy-start.7
  8.0 0.8 copy-done.7
  8.8 87.8 %shard_map.111 = (f32[64,256]{1,0:T(8,128)S(1)}, f32[64,256]{1,0:T(8,128)S(1)}, f32[64,256]{1,0:T(8,128)S(1)}, f32[64,256]{1,0:T(8,128)S(1)}) custom-call(bf16[8,64,256]{2,1,0:T(8,128)(2,1)S(1)} %copy-done.2, bf16[8,64,256]{2,1,0:T(8,128)(2,1)S(1)} %copy-done.3, bf16[64,256]{1,0:T(8,128)(2,1)S(1)} %bitcast.24, bf16[64,256]{1,0:T(8,128)(2,1)S(1)} %bitcast.25, ...), custom_call_target="tpu_custom_call" | custom-call | flops 536870912 | bytes 6291456 | tf_op jit(solution)/shard_map/pallas_call | solution.py:397
  96.6 0.6 copy.16
  97.2 0.6 copy.17
  97.8 0.6 copy.18
  98.5 0.6 copy.19
Async XLA Ops:
  0.6 1.6 %copy-start = (bf16[1,4096,256]{2,1,0:T(8,128)(2,1)S(1)}, bf16[1,4096,256]{2,1,0:T(8,128)(2,1)}, u32[]{:S(2)}) copy-start(bf16[1,4096,256]{2,1,0:T(8,128)(2,1)} %param.14) | copy-start | bytes 6291460
  2.2 1.6 %copy-start.1 = (bf16[1,4096,256]{2,1,0:T(8,128)(2,1)S(1)}, bf16[1,4096,256]{2,1,0:T(8,128)(2,1)}, u32[]{:S(2)}) copy-start(bf16[1,4096,256]{2,1,0:T(8,128)(2,1)} %param.15) | copy-start | bytes 6291460
  3.8 0.9 copy-start.2
  4.8 0.9 copy-start.3
  5.7 0.8 copy-start.4
  6.5 0.8 copy-start.5
  7.2 0.8 copy-start.6
  8.0 0.8 copy-start.7

commit v2 on v1

--- a/solution.py
+++ b/solution.py
@@ -43,11 +43,11 @@
 
 def kernel(
     xd, xu, atd, atu, bd, bu, wd, wu,
-    gad, gbd, gau, gbu,
-    w, weff, at, bch, hb, xs, xp, hout, eb, ps, pr, eout, gs, gr, cs, cr,
+    c_out, g_out, h_out, e_out,
+    w, weff, at, bch, hb, xs, xp, ts, tp, hout, eb, ps, pr, eout, gs, gr, cs, cr, fs, fr,
     ld_x, ld_a, ld_b, ld_w,
     w_s, w_r, b_s, b_r, a_s, a_r, h_s, h_r, hx_s, hx_r, hc_s, hc_r,
-    ec_s, ec_r, ex_s, ex_r, p_s, p_r, g_s, g_r, c_s, c_r,
+    ec_s, ec_r, ex_s, ex_r, p_s, p_r, g_s, g_r, c_s, c_r, t_s, t_r, f_s, f_r,
 ):
     sec, t = lax.axis_index("section"), lax.axis_index("tensor")
     group, s = sec // LAYERS, sec % LAYERS
@@ -128,11 +128,23 @@
             for m in FAR:
                 h_copy(0, i, m).start()
 
-    def share_weights(r):
+    def f_copy(m):
+        return remote(fs, fr.at[m], f_s.at[m], f_r.at[m], peer(m))
+
+    for r in range(2):
         pltpu.make_async_copy(atd, at.at[r, 0], ld_a.at[r]).wait()
+
+    @pl.when(q1 == 0)
+    def _():
+        fs[...] = fold(SCALE * nt(hb[0, 0], at[0, 0]))
+        for m in FAR:
+            f_copy(m).start()
+
+    def share_lower(r):
         for m in FAR:
             a_copy(r, m).start()
 
+    def share_weights(r):
         @pl.when(low == (r == 0))
         def _():
             w_copy(r, True).start()
@@ -145,12 +157,20 @@
         b_copy(r).start()
 
     share_weights(0)
+
+    @pl.when(q1 == 1)
+    def _():
+        share_lower(0)
+        share_lower(1)
+
     share_weights(1)
 
-    def combine_weights(r):
+    def weights_here(r):
         b_copy(r).wait_recv()
         pltpu.make_async_copy(wd.at[:, core], w.at[r, 0], ld_w.at[r]).wait()
         w_copy(r, True).wait_recv()
+
+    def combine_weights(r):
         for m in NEAR:
             if m:
                 a_copy(r, m).wait_recv()
@@ -182,34 +202,65 @@
             for m in FAR:
                 h_copy(r, i, m).start()
 
-    def forward(r):
-        own = []
-        for i in range(SPLIT):
+    def t_copy(i):
+        return remote(ts.at[rows(i)], tp.at[rows(i)], t_s.at[i], t_r.at[i], sibling)
+
+    def first_layer():
+        lower = fs[...]
+        for m in NEAR[1:]:
+            f_copy(m).wait_recv()
+            lower = lower + fr[m]
+        cs[0] = lower
+        c_copy(0).start()
+        c = unfold(lower).astype(BF16)
+        halves = []
+        for i in range(SPLIT):
+            piece = slice(i * ROWS, (i + 1) * ROWS)
+            own, other = nn(c[piece], bch[0, 0]), nn(c[piece], bch[0, 1])
+            for m in NEAR:
+                if m:
+                    h_copy(0, i, m).wait_recv()
+                other = other + nn(hb[0, m, piece], w[0, 1, chip ^ m])
+            xs[0, piece] = other
+            hx_copy(0, i).start()
+            for m in NEAR:
+                own = own + nn(hb[0, m, piece], w[0, 0, chip ^ m])
+            halves.append(own)
+        for i in range(SPLIT):
+            piece = slice(i * ROWS, (i + 1) * ROWS)
+            hx_copy(0, i).wait_recv()
+            out = (hb[0, 0, piece].astype(F32) + halves[i] + xp[0, piece]).astype(BF16)
+            hout[0, piece] = out
+            hc_copy(0, i).start()
+
+    def later_layer(r, last):
+        own, other = [], []
+        for i in range(SPLIT):
+            piece = slice(i * ROWS, (i + 1) * ROWS)
             total = jnp.zeros((ROWS, 2 * COLS), F32)
             for m in NEAR:
                 if m:
                     h_copy(r, i, m).wait_recv()
-                total = total + nn(hb[r, m, i * ROWS : (i + 1) * ROWS], weff[r, chip ^ m])
-            xs[r, i * ROWS : (i + 1) * ROWS] = total[:, COLS:]
+                total = total + nn(hb[r, m, piece], weff[r, chip ^ m])
+            xs[r, piece] = total[:, COLS:]
             hx_copy(r, i).start()
-            own.append(total[:, :COLS])
+            mine = hb[r, 0, piece].astype(F32) + total[:, :COLS]
+            if last:
+                ts[piece] = mine
+                t_copy(i).start()
+            own.append(mine)
+            other.append(total[:, COLS:])
         for i in range(SPLIT):
             piece = slice(i * ROWS, (i + 1) * ROWS)
             hx_copy(r, i).wait_recv()
-            out = (hb[r, 0, piece].astype(F32) + own[i] + xp[r, piece]).astype(BF16)
-            if r == 0:
+            out = (own[i] + xp[r, piece]).astype(BF16)
+            if last:
+                eb[r, 0, piece] = out
+                t_copy(i).wait_recv()
+                eb[r, 1, piece] = (other[i] + tp[piece]).astype(BF16)
+            else:
                 hout[r, piece] = out
                 hc_copy(r, i).start()
-            else:
-
-                @pl.when(q1 == 1)
-                def _():
-                    hout[r, piece] = out
-                    hc_copy(r, i).start()
-
-                @pl.when(q1 == 0)
-                def _():
-                    eb[r, 0, piece] = out
 
     def c_copy(r):
         return remote(cs.at[r], cr.at[r], c_s.at[r], c_r.at[r], sibling)
@@ -226,6 +277,12 @@
             for m in FAR:
                 h_copy(r, i, m).wait_send()
             hx_copy(r, i).wait_send()
+            if r == 1:
+
+                @pl.when(q1 == 0)
+                def _():
+                    t_copy(i).wait_send()
+
             if r == 0:
                 hc_copy(r, i).wait_send()
             else:
@@ -235,26 +292,45 @@
                     hc_copy(r, i).wait_send()
 
     def drain_weights(r):
-        for m in FAR:
-            a_copy(r, m).wait_send()
+        if r == 1:
+            for m in FAR:
+                a_copy(r, m).wait_send()
         b_copy(r).wait_send()
         w_copy(r, True).wait_send()
 
-    combine_weights(0)
+    weights_here(0)
+
+    @pl.when(q1 == 0)
+    def _():
+        first_layer()
+        share_lower(1)
+        for m in FAR:
+            f_copy(m).wait_send()
 
     @pl.when(q1 == 1)
     def _():
+        combine_weights(0)
         gather(0)
-
-    forward(0)
+        later_layer(0, False)
+        coefficients(0)
+        for m in FAR:
+            a_copy(0, m).wait_send()
+
+    weights_here(1)
     combine_weights(1)
-    coefficients(0)
     drain_weights(0)
     drain_weights(1)
     drain_forward(0)
 
     gather(1)
-    forward(1)
+
+    @pl.when(q1 == 0)
+    def _():
+        later_layer(1, True)
+
+    @pl.when(q1 == 1)
+    def _():
+        later_layer(1, False)
 
     def ec_copy(r, i):
         to = (sec - toward, t) if r == 0 else (sec + toward, t)
@@ -283,15 +359,10 @@
 
     def arrive(r):
         for i in range(SPLIT):
-            if r == 0:
-                ec_arrived(r, i)
-            else:
-
-                @pl.when(q1 == 1)
-                def _():
-                    ec_arrived(r, i)
-
+            ec_arrived(r, i)
             ex_copy(r, i).start()
+        for i in range(SPLIT):
+            ex_copy(r, i).wait_recv()
 
     def sum_g(r):
         total = nt(eb[r, 0], bch[r, 0]) + nt(eb[r, 1], bch[r, 1])
@@ -329,31 +400,19 @@
 
     def finish(r):
         c_copy(r).wait_recv()
-        c = unfold(cs[r] + cr[r]).astype(BF16)
-        grad_b = tn(c, eb[r, 0])
+        c_out[r] = unfold(cs[r] + cr[r]).astype(BF16)
+        h_out[r] = hb[r, 0]
+        e_out[r] = eb[r, 0]
         total = gs[r]
         for m in NEAR[1:]:
             g_copy(r, m).wait_recv()
             total = total + gr[r, m]
-        g = unfold(total).astype(BF16)
-        grad_a = SCALE * tn(g, hb[r, 0])
-
-        @pl.when(low == (r == 0))
-        def _():
-            gad[...] = grad_a
-            gbd[...] = grad_b
-
-        @pl.when(low != (r == 0))
-        def _():
-            gau[...] = grad_a
-            gbu[...] = grad_b
-
-    def arrived_other(r):
-        for i in range(SPLIT):
-            ex_copy(r, i).wait_recv()
-
-    arrive(1)
-    arrived_other(1)
+        g_out[r] = unfold(total).astype(BF16)
+
+    @pl.when(q1 == 1)
+    def _():
+        arrive(1)
+
     backward(1)
     sum_g(1)
     coefficients(1)
@@ -362,7 +421,6 @@
     drain_backward(1)
 
     arrive(0)
-    arrived_other(0)
 
     @pl.when(q1 == 1)
     def _():
@@ -374,29 +432,45 @@
     @pl.when(q1 == 1)
     def _():
         drain_backward(0)
-
+        for i in range(SPLIT):
+            ex_copy(1, i).wait_send()
+
+    for i in range(SPLIT):
+        ex_copy(0, i).wait_send()
     for r in range(2):
-        for i in range(SPLIT):
-            ex_copy(r, i).wait_send()
         for m in FAR:
             g_copy(r, m).wait_send()
         c_copy(r).wait_send()
 
 
+def gradients(c, g, h, e, gad, gbd, gau, gbu):
+    low = lax.axis_index("section") % LAYERS < 2
+    grad_a = [SCALE * tn(g[r], h[r]) for r in range(2)]
+    grad_b = [tn(c[r], e[r]) for r in range(2)]
+
+    @pl.when(low)
+    def _():
+        gad[...], gbd[...], gau[...], gbu[...] = grad_a[0], grad_b[0], grad_a[1], grad_b[1]
+
+    @pl.when(jnp.logical_not(low))
+    def _():
+        gad[...], gbd[...], gau[...], gbu[...] = grad_a[1], grad_b[1], grad_a[0], grad_b[0]
+
+
 def body(xd, xu, ad, bd, au, bu, wd, wu):
     def chunks(v):
         return v.reshape(CHIPS, 2, COLS, COLS)
 
     dma = pltpu.SemaphoreType.DMA
-    anywhere = pl.BlockSpec(memory_space=pl.ANY)
+    anywhere = pl.BlockSpec(memory_space=pltpu.HBM)
     vmem = pl.BlockSpec(memory_space=pltpu.VMEM)
     pair = dma((2,))
     halves = dma((2, SPLIT))
     each = dma((2, SPLIT, CHIPS))
     chips = dma((2, CHIPS))
-    gad, gbd, gau, gbu = pl.pallas_call(
+    parts = pl.pallas_call(
         kernel,
-        out_shape=[jax.ShapeDtypeStruct((RANK, COLS), F32)] * 4,
+        out_shape=[jax.ShapeDtypeStruct((2, TOK, n), BF16) for n in (RANK, RANK, COLS, COLS)],
         in_specs=[anywhere] * 8,
         out_specs=[vmem] * 4,
         scratch_shapes=[
@@ -407,6 +481,8 @@
             pltpu.VMEM((2, CHIPS, TOK, COLS), BF16),
             pltpu.VMEM((2, TOK, COLS), F32),
             pltpu.VMEM((2, TOK, COLS), F32),
+            pltpu.VMEM((TOK, COLS), F32),
+            pltpu.VMEM((TOK, COLS), F32),
             pltpu.VMEM((2, TOK, COLS), BF16),
             pltpu.VMEM((2, 2, TOK, COLS), BF16),
             pltpu.VMEM((2, CHIPS, TOK, COLS), BF16),
@@ -416,14 +492,17 @@
             pltpu.VMEM((2, CHIPS, TOK // 2, 2 * RANK), F32),
             pltpu.VMEM((2, TOK // 2, 2 * RANK), F32),
             pltpu.VMEM((2, TOK // 2, 2 * RANK), F32),
+            pltpu.VMEM((TOK // 2, 2 * RANK), F32),
+            pltpu.VMEM((CHIPS, TOK // 2, 2 * RANK), F32),
             dma, pair, pair, pair,
             pair, pair, pair, pair, chips, chips,
             each, each, halves, halves, halves, halves,
             halves, halves, halves, halves,
             each, each, chips, chips, pair, pair,
+            dma((SPLIT,)), dma((SPLIT,)), dma((CHIPS,)), dma((CHIPS,)),
         ],
         compiler_params=pltpu.CompilerParams(
-            collective_id=0, has_side_effects=True, vmem_limit_bytes=40 * 2**20
+            collective_id=0, has_side_effects=True, vmem_limit_bytes=62 * 2**20
         ),
         cost_estimate=pl.CostEstimate(
             flops=8 * TOK * LAYERS * 1024 * COLS, bytes_accessed=6 * 2**20, transcendentals=0
@@ -431,6 +510,13 @@
     )(
         xd, xu, ad[0].T, au[0].T, bd[0], bu[0], chunks(wd), chunks(wu)
     )
+    gad, gbd, gau, gbu = pl.pallas_call(
+        gradients,
+        out_shape=[jax.ShapeDtypeStruct((RANK, COLS), F32)] * 4,
+        in_specs=[vmem] * 4,
+        out_specs=[vmem] * 4,
+        compiler_params=pltpu.CompilerParams(vmem_limit_bytes=62 * 2**20),
+    )(*parts)
     return gad.T[None], gbd[None], gau.T[None], gbu[None]
 
 

time: 99.6 us -> 86.1 us (0.86)
  local copies, waits for them, and re-layouts: 10.6 us -> 0 us
  Pallas kernels: 87.8 us -> 85.2 us
    unnamed x20 -> x0, local copies, waits for them, and re-layouts: 10.6 us -> none
    pallas_call x1 -> x2, Pallas kernels: 87.8 us -> 85.2 us  [the longest x1 83.4 us: body(): pl.pallas_call(kernel, out_shape=[jax.ShapeDtypeStruct((2, TOK, n), BF16)...]
where the time goes in v2:
time: 86.1 us; the launch traced here: 85.9 us
  Pallas kernels  85.2 us (99%)
    pallas_call x1, Pallas kernels, body(): pl.pallas_call(kernel, out_shape=[jax.ShapeDtypeStruct((2, TOK, n), BF16)...  83.4 us
    pallas_call x1, Pallas kernels, body(): pl.pallas_call(gradients, out_shape=[jax.ShapeDtypeStruct((RANK, COLS), F...  1.83 us

profile of v2, /device:TPU:1, one launch (start us, length us, event | category | flops | bytes accessed | tf_op | source)
XLA Modules:
  0.0 85.9 jit_solution(7820494912152012630)
XLA Ops:
  0.6 83.4 %shard_map.111 = (bf16[2,64,64]{2,1,0:T(8,128)(2,1)}, bf16[2,64,64]{2,1,0:T(8,128)(2,1)}, bf16[2,64,256]{2,1,0:T(8,128)(2,1)}, bf16[2,64,256]{2,1,0:T(8,128)(2,1)}) custom-call(bf16[8,64,256]{2,1,0:T(8,128)(2,1)} %xd.1, bf16[8,64,256]{2,1,0:T(8,128)(2,1)} %xu.1, bf16[64,256]{1,0:T(8,128)(2,1)} %bitcast.20, bf16[64,256]{1,0:T(8,128)(2,1)} %bitcast.21, ...), custom_call_target="tpu_custom_call" | custom-call | flops 536870912 | bytes 6291456 | tf_op jit(solution)/shard_map/pallas_call | solution.py:471
  84.1 1.8 %shard_map.112 = (f32[64,256]{1,0:T(8,128)}, f32[64,256]{1,0:T(8,128)}, f32[64,256]{1,0:T(8,128)}, f32[64,256]{1,0:T(8,128)}) custom-call(bf16[2,64,64]{2,1,0:T(8,128)(2,1)} %get-tuple-element.12.c, bf16[2,64,64]{2,1,0:T(8,128)(2,1)} %get-tuple-element.13.g, bf16[2,64,256]{2,1,0:T(8,128)(2,1)} %get-tuple-element.14.h, bf16[2,64,256]{2,1,0:T(8,128)(2,1)} %get-tuple-element.15.e), custom_call_target="tpu_custom_call" | custom-call | tf_op jit(solution)/shard_map/pallas_call | solution.py:513

commit v3 on v2

--- a/solution.py
+++ b/solution.py
@@ -19,6 +19,7 @@
 SCALE = 2.0
 FAR = (5, 4, 7, 3, 6, 2, 1)
 NEAR = (0, 1, 2, 6, 3, 7, 4, 5)
+WIDE = (11, 10, 9, 8, 15, 14, 7, 6, 13, 12, 5, 4, 3, 2, 1)
 
 
 def nn(a, b):
@@ -45,9 +46,11 @@
     xd, xu, atd, atu, bd, bu, wd, wu,
     c_out, g_out, h_out, e_out,
     w, weff, at, bch, hb, xs, xp, ts, tp, hout, eb, ps, pr, eout, gs, gr, cs, cr, fs, fr,
+    kept, b0, bp, us, ur, vs, vr,
     ld_x, ld_a, ld_b, ld_w,
     w_s, w_r, b_s, b_r, a_s, a_r, h_s, h_r, hx_s, hx_r, hc_s, hc_r,
     ec_s, ec_r, ex_s, ex_r, p_s, p_r, g_s, g_r, c_s, c_r, t_s, t_r, f_s, f_r,
+    n_s, n_r, m_s, m_r, u_s, u_r, v_s, v_r,
 ):
     sec, t = lax.axis_index("section"), lax.axis_index("tensor")
     group, s = sec // LAYERS, sec % LAYERS
@@ -213,7 +216,6 @@
         cs[0] = lower
         c_copy(0).start()
         c = unfold(lower).astype(BF16)
-        halves = []
         for i in range(SPLIT):
             piece = slice(i * ROWS, (i + 1) * ROWS)
             own, other = nn(c[piece], bch[0, 0]), nn(c[piece], bch[0, 1])
@@ -225,42 +227,33 @@
             hx_copy(0, i).start()
             for m in NEAR:
                 own = own + nn(hb[0, m, piece], w[0, 0, chip ^ m])
-            halves.append(own)
-        for i in range(SPLIT):
-            piece = slice(i * ROWS, (i + 1) * ROWS)
+            own = own + hb[0, 0, piece].astype(F32)
             hx_copy(0, i).wait_recv()
-            out = (hb[0, 0, piece].astype(F32) + halves[i] + xp[0, piece]).astype(BF16)
-            hout[0, piece] = out
+            hout[0, piece] = (own + xp[0, piece]).astype(BF16)
             hc_copy(0, i).start()
 
-    def later_layer(r, last):
-        own, other = [], []
-        for i in range(SPLIT):
-            piece = slice(i * ROWS, (i + 1) * ROWS)
-            total = jnp.zeros((ROWS, 2 * COLS), F32)
-            for m in NEAR:
-                if m:
-                    h_copy(r, i, m).wait_recv()
-                total = total + nn(hb[r, m, piece], weff[r, chip ^ m])
-            xs[r, piece] = total[:, COLS:]
-            hx_copy(r, i).start()
-            mine = hb[r, 0, piece].astype(F32) + total[:, :COLS]
-            if last:
-                ts[piece] = mine
-                t_copy(i).start()
-            own.append(mine)
-            other.append(total[:, COLS:])
-        for i in range(SPLIT):
-            piece = slice(i * ROWS, (i + 1) * ROWS)
-            hx_copy(r, i).wait_recv()
-            out = (own[i] + xp[r, piece]).astype(BF16)
-            if last:
-                eb[r, 0, piece] = out
-                t_copy(i).wait_recv()
-                eb[r, 1, piece] = (other[i] + tp[piece]).astype(BF16)
-            else:
-                hout[r, piece] = out
-                hc_copy(r, i).start()
+    def later_layer(r, i, last):
+        piece = slice(i * ROWS, (i + 1) * ROWS)
+        total = jnp.zeros((ROWS, 2 * COLS), F32)
+        for m in NEAR:
+            if m:
+                h_copy(r, i, m).wait_recv()
+            total = total + nn(hb[r, m, piece], weff[r, chip ^ m])
+        xs[r, piece] = total[:, COLS:]
+        hx_copy(r, i).start()
+        mine = hb[r, 0, piece].astype(F32) + total[:, :COLS]
+        if last:
+            ts[piece] = mine
+            t_copy(i).start()
+        hx_copy(r, i).wait_recv()
+        out = (mine + xp[r, piece]).astype(BF16)
+        if last:
+            eb[r, 0, piece] = out
+            t_copy(i).wait_recv()
+            eb[r, 1, piece] = (total[:, COLS:] + tp[piece]).astype(BF16)
+        else:
+            hout[r, piece] = out
+            hc_copy(r, i).start()
 
     def c_copy(r):
         return remote(cs.at[r], cr.at[r], c_s.at[r], c_r.at[r], sibling)
@@ -298,40 +291,6 @@
         b_copy(r).wait_send()
         w_copy(r, True).wait_send()
 
-    weights_here(0)
-
-    @pl.when(q1 == 0)
-    def _():
-        first_layer()
-        share_lower(1)
-        for m in FAR:
-            f_copy(m).wait_send()
-
-    @pl.when(q1 == 1)
-    def _():
-        combine_weights(0)
-        gather(0)
-        later_layer(0, False)
-        coefficients(0)
-        for m in FAR:
-            a_copy(0, m).wait_send()
-
-    weights_here(1)
-    combine_weights(1)
-    drain_weights(0)
-    drain_weights(1)
-    drain_forward(0)
-
-    gather(1)
-
-    @pl.when(q1 == 0)
-    def _():
-        later_layer(1, True)
-
-    @pl.when(q1 == 1)
-    def _():
-        later_layer(1, False)
-
     def ec_copy(r, i):
         to = (sec - toward, t) if r == 0 else (sec + toward, t)
         there = 0 if r == 0 else 1 - q1
@@ -357,40 +316,38 @@
     def g_copy(r, m):
         return remote(gs.at[r], gr.at[r, m], g_s.at[r, m], g_r.at[r, m], peer(m))
 
-    def arrive(r):
-        for i in range(SPLIT):
-            ec_arrived(r, i)
-            ex_copy(r, i).start()
-        for i in range(SPLIT):
-            ex_copy(r, i).wait_recv()
-
     def sum_g(r):
         total = nt(eb[r, 0], bch[r, 0]) + nt(eb[r, 1], bch[r, 1])
         gs[r] = fold(total)
         for m in FAR:
             g_copy(r, m).start()
 
-    def backward(r):
-        own = []
-        for i in range(SPLIT):
-            piece = slice(i * ROWS, (i + 1) * ROWS)
-            e_own, e_other = eb[r, 0, piece], eb[r, 1, piece]
-            for m in FAR + (0,):
-                block = weff.at[r, chip ^ m]
-                part = nt(e_own, block[:, :COLS]) + nt(e_other, block[:, COLS:])
-                if m:
-                    ps[r, m, piece] = part.astype(BF16)
-                    p_copy(r, i, m).start()
-                else:
-                    own.append(part)
-        for i in range(SPLIT):
-            piece = slice(i * ROWS, (i + 1) * ROWS)
-            total = eb[r, 0, piece].astype(F32) + own[i]
-            for m in NEAR[1:]:
-                p_copy(r, i, m).wait_recv()
-                total = total + pr[r, m, piece].astype(F32)
-            eout[r, piece] = total.astype(BF16)
-            ec_copy(r, i).start()
+    def backward_out(r, i, turn):
+        piece = slice(i * ROWS, (i + 1) * ROWS)
+        if not turn:
+            ec_arrived(r, i)
+            ex_copy(r, i).start()
+        e_own = eb[r, 0, piece]
+        parts = [nt(e_own, weff[r, chip ^ m, :, :COLS]) for m in FAR + (0,)]
+        if not turn:
+            ex_copy(r, i).wait_recv()
+        e_other = eb[r, 1, piece]
+        for m, part in zip(FAR + (0,), parts):
+            part = part + nt(e_other, weff[r, chip ^ m, :, COLS:])
+            if m:
+                ps[r, m, piece] = part.astype(BF16)
+                p_copy(r, i, m).start()
+            else:
+                kept[r, piece] = part + e_own.astype(F32)
+
+    def backward_in(r, i):
+        piece = slice(i * ROWS, (i + 1) * ROWS)
+        total = kept[r, piece]
+        for m in NEAR[1:]:
+            p_copy(r, i, m).wait_recv()
+            total = total + pr[r, m, piece].astype(F32)
+        eout[r, piece] = total.astype(BF16)
+        ec_copy(r, i).start()
 
     def drain_backward(r):
         for i in range(SPLIT):
@@ -398,48 +355,142 @@
                 p_copy(r, i, m).wait_send()
             ec_copy(r, i).wait_send()
 
-    def finish(r):
+    def n_copy():
+        return remote(bch.at[0, 0], b0.at[0], n_s, n_r, (sec + toward, t))
+
+    def m_copy(m):
+        return remote(b0.at[0], b0.at[m], m_s.at[m], m_r.at[m], peer(m))
+
+    def u_copy():
+        return remote(us, ur, u_s, u_r, (sec - toward, t))
+
+    def v_copy(n):
+        return remote(vs, vr.at[n], v_s.at[n], v_r.at[n], (sec, t ^ n))
+
+    def prepare_ahead():
+        remote(bch.at[0, 0], b0.at[0], n_s, n_r, sibling).wait_recv()
+        for m in FAR:
+            m_copy(m).start()
+        own, other = b0[0].astype(F32), jnp.zeros((RANK, COLS), F32)
+        for m in NEAR:
+            if m:
+                m_copy(m).wait_recv()
+            own = own + nn(b0[m], weff[0, chip ^ m, :, :COLS])
+            other = other + nn(b0[m], weff[0, chip ^ m, :, COLS:])
+        bp[0] = own.astype(BF16)
+        bp[1] = other.astype(BF16)
+        for m in FAR:
+            m_copy(m).wait_send()
+
+    def send_ahead():
+        us[...] = fold(nt(eb[0, 0], bp[0]) + nt(eb[0, 1], bp[1]))
+        u_copy().start()
+
+    def receive_ahead():
+        remote(us, ur, u_s, u_r, sibling).wait_recv()
+        vs[...] = ur[...].astype(BF16)
+        for n in WIDE:
+            v_copy(n).start()
+        total = ur[...]
+        for n in reversed(WIDE):
+            v_copy(n).wait_recv()
+            total = total + vr[n].astype(F32)
+        g_out[0] = unfold(total).astype(BF16)
+
+    def keep(r):
         c_copy(r).wait_recv()
         c_out[r] = unfold(cs[r] + cr[r]).astype(BF16)
         h_out[r] = hb[r, 0]
-        e_out[r] = eb[r, 0]
+
+    def finish(r):
         total = gs[r]
         for m in NEAR[1:]:
             g_copy(r, m).wait_recv()
             total = total + gr[r, m]
         g_out[r] = unfold(total).astype(BF16)
+        e_out[r] = eb[r, 0]
+
+    def close_forward():
+        drain_weights(0)
+        drain_weights(1)
+        drain_forward(0)
+        keep(0)
+
+    def close_backward(r):
+        finish(r)
+        drain_backward(r)
+        for m in FAR:
+            g_copy(r, m).wait_send()
+
+    @pl.when(q1 == 0)
+    def _():
+        weights_here(0)
+        first_layer()
+        n_copy().start()
+        share_lower(1)
+        for m in FAR:
+            f_copy(m).wait_send()
+        weights_here(1)
+        combine_weights(1)
+        n_copy().wait_send()
+        close_forward()
+        gather(1)
+        for i in range(SPLIT):
+            later_layer(1, i, True)
+            backward_out(1, i, True)
+        for i in range(SPLIT):
+            backward_in(1, i)
+        sum_g(1)
+        coefficients(1)
+        drain_forward(1)
+        keep(1)
+        close_backward(1)
+        receive_ahead()
+        for n in WIDE:
+            v_copy(n).wait_send()
+        for i in range(SPLIT):
+            ec_arrived(0, i)
+        e_out[0] = eb[0, 0]
 
     @pl.when(q1 == 1)
     def _():
-        arrive(1)
-
-    backward(1)
-    sum_g(1)
-    coefficients(1)
-    drain_forward(1)
-    finish(1)
-    drain_backward(1)
-
-    arrive(0)
-
-    @pl.when(q1 == 1)
-    def _():
-        backward(0)
-
-    sum_g(0)
-    finish(0)
-
-    @pl.when(q1 == 1)
-    def _():
-        drain_backward(0)
-        for i in range(SPLIT):
-            ex_copy(1, i).wait_send()
-
-    for i in range(SPLIT):
-        ex_copy(0, i).wait_send()
+        weights_here(0)
+        combine_weights(0)
+        gather(0)
+        weights_here(1)
+        combine_weights(1)
+        for i in range(SPLIT):
+            later_layer(0, i, False)
+        gather(1)
+        coefficients(0)
+        for m in FAR:
+            a_copy(0, m).wait_send()
+        close_forward()
+        for i in range(SPLIT):
+            later_layer(1, i, False)
+        prepare_ahead()
+        coefficients(1)
+        drain_forward(1)
+        keep(1)
+        for i in range(SPLIT):
+            backward_out(1, i, False)
+        for i in range(SPLIT):
+            backward_in(1, i)
+        sum_g(1)
+        for i in range(SPLIT):
+            backward_out(0, i, False)
+        send_ahead()
+        close_backward(1)
+        for i in range(SPLIT):
+            backward_in(0, i)
+        sum_g(0)
+        close_backward(0)
+        for r in range(2):
+            for i in range(SPLIT):
+                ex_copy(r, i).wait_send()
+        u_copy().wait_send()
+
     for r in range(2):
-        for m in FAR:
-            g_copy(r, m).wait_send()
         c_copy(r).wait_send()
 
 
@@ -494,12 +545,20 @@
             pltpu.VMEM((2, TOK // 2, 2 * RANK), F32),
             pltpu.VMEM((TOK // 2, 2 * RANK), F32),
             pltpu.VMEM((CHIPS, TOK // 2, 2 * RANK), F32),
+            pltpu.VMEM((2, TOK, COLS), F32),
+            pltpu.VMEM((CHIPS, RANK, COLS), BF16),
+            pltpu.VMEM((2, RANK, COLS), BF16),
+            pltpu.VMEM((TOK // 2, 2 * RANK), F32),
+            pltpu.VMEM((TOK // 2, 2 * RANK), F32),
+            pltpu.VMEM((TOK // 2, 2 * RANK), BF16),
+            pltpu.VMEM((2 * CHIPS, TOK // 2, 2 * RANK), BF16),
             dma, pair, pair, pair,
             pair, pair, pair, pair, chips, chips,
             each, each, halves, halves, halves, halves,
             halves, halves, halves, halves,
             each, each, chips, chips, pair, pair,
             dma((SPLIT,)), dma((SPLIT,)), dma((CHIPS,)), dma((CHIPS,)),
+            dma, dma, dma((CHIPS,)), dma((CHIPS,)), dma, dma, dma((2 * CHIPS,)), dma((2 * CHIPS,)),
         ],
         compiler_params=pltpu.CompilerParams(
             collective_id=0, has_side_effects=True, vmem_limit_bytes=62 * 2**20

time: 86.1 us -> 79.6 us (0.925)
  Pallas kernels: 85.2 us -> 78.8 us
    pallas_call x1, Pallas kernels: 83.4 us -> 77 us  [body(): pl.pallas_call(kernel, out_shape=[jax.ShapeDtypeStruct((2, TOK, n), BF16)...]
where the time goes in v3:
time: 79.6 us; the launch traced here: 79.4 us
  Pallas kernels  78.8 us (99%)
    pallas_call x1, Pallas kernels, body(): pl.pallas_call(kernel, out_shape=[jax.ShapeDtypeStruct((2, TOK, n), BF16)...  77 us
    pallas_call x1, Pallas kernels, body(): pl.pallas_call(gradients, out_shape=[jax.ShapeDtypeStruct((RANK, COLS), F...  1.83 us

profile of v3, /device:TPU:1, one launch (start us, length us, event | category | flops | bytes accessed | tf_op | source)
XLA Modules:
  0.0 79.4 jit_solution(12531890079415517558)
XLA Ops:
  0.6 77.0 %shard_map.111 = (bf16[2,64,64]{2,1,0:T(8,128)(2,1)}, bf16[2,64,64]{2,1,0:T(8,128)(2,1)}, bf16[2,64,256]{2,1,0:T(8,128)(2,1)}, bf16[2,64,256]{2,1,0:T(8,128)(2,1)}) custom-call(bf16[8,64,256]{2,1,0:T(8,128)(2,1)} %xd.1, bf16[8,64,256]{2,1,0:T(8,128)(2,1)} %xu.1, bf16[64,256]{1,0:T(8,128)(2,1)} %bitcast.20, bf16[64,256]{1,0:T(8,128)(2,1)} %bitcast.21, ...), custom_call_target="tpu_custom_call" | custom-call | flops 536870912 | bytes 6291456 | tf_op jit(solution)/shard_map/pallas_call | solution.py:522
  77.6 1.8 %shard_map.112 = (f32[64,256]{1,0:T(8,128)}, f32[64,256]{1,0:T(8,128)}, f32[64,256]{1,0:T(8,128)}, f32[64,256]{1,0:T(8,128)}) custom-call(bf16[2,64,64]{2,1,0:T(8,128)(2,1)} %get-tuple-element.12.c, bf16[2,64,64]{2,1,0:T(8,128)(2,1)} %get-tuple-element.13.g, bf16[2,64,256]{2,1,0:T(8,128)(2,1)} %get-tuple-element.14.h, bf16[2,64,256]{2,1,0:T(8,128)(2,1)} %get-tuple-element.15.e), custom_call_target="tpu_custom_call" | custom-call | tf_op jit(solution)/shard_map/pallas_call | solution.py:572

commit v4 on v3

--- a/solution.py
+++ b/solution.py
@@ -17,8 +17,8 @@
 SPLIT = 2
 ROWS = TOK // SPLIT
 SCALE = 2.0
-FAR = (5, 4, 7, 3, 6, 2, 1)
-NEAR = (0, 1, 2, 6, 3, 7, 4, 5)
+FAR = (5, 7, 3, 4, 6, 2, 1)
+NEAR = (0, 5, 7, 3, 4, 6, 2, 1)
 WIDE = (11, 10, 9, 8, 15, 14, 7, 6, 13, 12, 5, 4, 3, 2, 1)
 
 
@@ -45,7 +45,7 @@
 def kernel(
     xd, xu, atd, atu, bd, bu, wd, wu,
     c_out, g_out, h_out, e_out,
-    w, weff, at, bch, hb, xs, xp, ts, tp, hout, eb, ps, pr, eout, gs, gr, cs, cr, fs, fr,
+    w, weff, at, bch, hb, xs, xp, ts, tp, hs, hin, eb, ps, pr, eout, gs, gr, cs, cr, fs, fr,
     kept, b0, bp, us, ur, vs, vr,
     ld_x, ld_a, ld_b, ld_w,
     w_s, w_r, b_s, b_r, a_s, a_r, h_s, h_r, hx_s, hx_r, hc_s, hc_r,
@@ -72,6 +72,21 @@
             device_id=to, device_id_type=MESH,
         )
 
+    barrier = pltpu.get_barrier_semaphore()
+    for m in FAR:
+        pl.semaphore_signal(barrier, inc=1, device_id=peer(m), device_id_type=MESH)
+    pl.semaphore_signal(barrier, inc=1, device_id=sibling, device_id_type=MESH)
+
+    @pl.when(s > 0)
+    def _():
+        for other in (t, t ^ 1):
+            pl.semaphore_signal(barrier, inc=1, device_id=(sec - 1, other), device_id_type=MESH)
+
+    @pl.when(s < LAYERS - 1)
+    def _():
+        for other in (t, t ^ 1):
+            pl.semaphore_signal(barrier, inc=1, device_id=(sec + 1, other), device_id_type=MESH)
+
     def start_local(r, down):
         x, a, b, v = (xd, atd, bd, wd) if down else (xu, atu, bu, wu)
         if r == 0:
@@ -94,20 +109,7 @@
         start_local(0, False)
         start_local(1, True)
 
-    barrier = pltpu.get_barrier_semaphore()
-    for m in range(1, CHIPS):
-        pl.semaphore_signal(barrier, inc=1, device_id=peer(m), device_id_type=MESH)
-    pl.semaphore_signal(barrier, inc=1, device_id=sibling, device_id_type=MESH)
-
-    @pl.when(s > 0)
-    def _():
-        pl.semaphore_signal(barrier, inc=1, device_id=(sec - 1, t), device_id_type=MESH)
-
-    @pl.when(s < LAYERS - 1)
-    def _():
-        pl.semaphore_signal(barrier, inc=1, device_id=(sec + 1, t), device_id_type=MESH)
-
-    pl.semaphore_wait(barrier, jnp.where(q1 == 0, CHIPS + 1, CHIPS + 2))
+    pl.semaphore_wait(barrier, jnp.where(q1 == 0, CHIPS + 2, CHIPS + 4))
 
     def h_copy(r, i, m):
         return remote(
@@ -127,21 +129,23 @@
     @pl.when(q1 == 0)
     def _():
         pltpu.make_async_copy(xd.at[group], hb.at[0, 0], ld_x).wait()
-        for i in range(SPLIT):
+        for m in FAR:
+            h_copy(0, 0, m).start()
+
+    def f_copy(m):
+        return remote(fs, fr.at[m], f_s.at[m], f_r.at[m], peer(m))
+
+    for r in range(2):
+        pltpu.make_async_copy(atd, at.at[r, 0], ld_a.at[r]).wait()
+
+    @pl.when(q1 == 0)
+    def _():
+        fs[...] = fold(SCALE * nt(hb[0, 0], at[0, 0]))
+        for m in FAR:
+            f_copy(m).start()
+        for i in range(1, SPLIT):
             for m in FAR:
                 h_copy(0, i, m).start()
-
-    def f_copy(m):
-        return remote(fs, fr.at[m], f_s.at[m], f_r.at[m], peer(m))
-
-    for r in range(2):
-        pltpu.make_async_copy(atd, at.at[r, 0], ld_a.at[r]).wait()
-
-    @pl.when(q1 == 0)
-    def _():
-        fs[...] = fold(SCALE * nt(hb[0, 0], at[0, 0]))
-        for m in FAR:
-            f_copy(m).start()
 
     def share_lower(r):
         for m in FAR:
@@ -164,9 +168,8 @@
     @pl.when(q1 == 1)
     def _():
         share_lower(0)
+        share_weights(1)
         share_lower(1)
-
-    share_weights(1)
 
     def weights_here(r):
         b_copy(r).wait_recv()
@@ -184,20 +187,31 @@
                     w[r, half, j].astype(F32) + SCALE * low_rank
                 ).astype(BF16)
 
-    def hx_copy(r, i):
-        return remote(xs.at[r, rows(i)], xp.at[r, rows(i)], hx_s.at[r, i], hx_r.at[r, i], sibling)
-
-    def hc_copy(r, i):
-        to = (sec + toward, t) if r == 0 else (sec - toward, t)
+    def hx_copy(i):
+        return remote(xs.at[rows(i)], xp.at[rows(i)], hx_s.at[i], hx_r.at[i], sibling)
+
+    def hc_copy(r, i, half):
+        to = (sec + toward if r == 0 else sec - toward, t ^ half)
         there = q1 if r == 0 else 1
         return remote(
-            hout.at[r, rows(i)], hb.at[there, 0, rows(i)], hc_s.at[r, i], hc_r.at[there, i], to
+            hs.at[r, half, rows(i)], hin.at[there, half, rows(i)],
+            hc_s.at[r, half, i], hc_r.at[there, half, i], to,
         )
 
     def hc_arrived(r, i):
-        remote(
-            hout.at[r, rows(i)], hb.at[r, 0, rows(i)], hc_s.at[r, i], hc_r.at[r, i], sibling
-        ).wait_recv()
+        for half in range(2):
+            remote(
+                hs.at[r, half, rows(i)], hin.at[r, half, rows(i)],
+                hc_s.at[r, half, i], hc_r.at[r, half, i], sibling,
+            ).wait_recv()
+        piece = slice(i * ROWS, (i + 1) * ROWS)
+        hb[r, 0, piece] = (
+            hin[r, 0, piece].astype(F32) + hin[r, 1, piece].astype(F32)
+        ).astype(BF16)
+
+    def cross(r, i, half, value):
+        hs[r, half, i * ROWS : (i + 1) * ROWS] = value.astype(BF16)
+        hc_copy(r, i, half).start()
 
     def gather(r):
         for i in range(SPLIT):
@@ -209,28 +223,27 @@
         return remote(ts.at[rows(i)], tp.at[rows(i)], t_s.at[i], t_r.at[i], sibling)
 
     def first_layer():
-        lower = fs[...]
-        for m in NEAR[1:]:
-            f_copy(m).wait_recv()
-            lower = lower + fr[m]
-        cs[0] = lower
-        c_copy(0).start()
-        c = unfold(lower).astype(BF16)
         for i in range(SPLIT):
             piece = slice(i * ROWS, (i + 1) * ROWS)
-            own, other = nn(c[piece], bch[0, 0]), nn(c[piece], bch[0, 1])
+            other = jnp.zeros((ROWS, COLS), F32)
             for m in NEAR:
                 if m:
                     h_copy(0, i, m).wait_recv()
                 other = other + nn(hb[0, m, piece], w[0, 1, chip ^ m])
-            xs[0, piece] = other
-            hx_copy(0, i).start()
+            if i == 0:
+                lower = fs[...]
+                for m in NEAR[1:]:
+                    f_copy(m).wait_recv()
+                    lower = lower + fr[m]
+                cs[0] = lower
+                c = unfold(lower).astype(BF16)
+            other = other + nn(c[piece], bch[0, 1])
+            cross(0, i, 1, other)
+            own = nn(c[piece], bch[0, 0])
             for m in NEAR:
                 own = own + nn(hb[0, m, piece], w[0, 0, chip ^ m])
-            own = own + hb[0, 0, piece].astype(F32)
-            hx_copy(0, i).wait_recv()
-            hout[0, piece] = (own + xp[0, piece]).astype(BF16)
-            hc_copy(0, i).start()
+            cross(0, i, 0, own + hb[0, 0, piece].astype(F32))
+        c_copy(0).start()
 
     def later_layer(r, i, last):
         piece = slice(i * ROWS, (i + 1) * ROWS)
@@ -239,21 +252,19 @@
             if m:
                 h_copy(r, i, m).wait_recv()
             total = total + nn(hb[r, m, piece], weff[r, chip ^ m])
-        xs[r, piece] = total[:, COLS:]
-        hx_copy(r, i).start()
         mine = hb[r, 0, piece].astype(F32) + total[:, :COLS]
-        if last:
-            ts[piece] = mine
-            t_copy(i).start()
-        hx_copy(r, i).wait_recv()
-        out = (mine + xp[r, piece]).astype(BF16)
-        if last:
-            eb[r, 0, piece] = out
-            t_copy(i).wait_recv()
-            eb[r, 1, piece] = (total[:, COLS:] + tp[piece]).astype(BF16)
-        else:
-            hout[r, piece] = out
-            hc_copy(r, i).start()
+        if not last:
+            cross(r, i, 0, mine)
+            cross(r, i, 1, total[:, COLS:])
+            return
+        xs[piece] = total[:, COLS:]
+        hx_copy(i).start()
+        ts[piece] = mine
+        t_copy(i).start()
+        hx_copy(i).wait_recv()
+        eb[r, 0, piece] = (mine + xp[piece]).astype(BF16)
+        t_copy(i).wait_recv()
+        eb[r, 1, piece] = (total[:, COLS:] + tp[piece]).astype(BF16)
 
     def c_copy(r):
         return remote(cs.at[r], cr.at[r], c_s.at[r], c_r.at[r], sibling)
@@ -265,24 +276,16 @@
         cs[r] = fold(SCALE * total)
         c_copy(r).start()
 
-    def drain_forward(r):
+    def drain_forward(r, last=False):
         for i in range(SPLIT):
             for m in FAR:
                 h_copy(r, i, m).wait_send()
-            hx_copy(r, i).wait_send()
-            if r == 1:
-
-                @pl.when(q1 == 0)
-                def _():
-                    t_copy(i).wait_send()
-
-            if r == 0:
-                hc_copy(r, i).wait_send()
+            if last:
+                hx_copy(i).wait_send()
+                t_copy(i).wait_send()
             else:
-
-                @pl.when(q1 == 1)
-                def _():
-                    hc_copy(r, i).wait_send()
+                for half in range(2):
+                    hc_copy(r, i, half).wait_send()
 
     def drain_weights(r):
         if r == 1:
@@ -303,10 +306,16 @@
             eout.at[r, rows(i)], eb.at[r, 0, rows(i)], ec_s.at[r, i], ec_r.at[r, i], sibling
         ).wait_recv()
 
-    def ex_copy(r, i):
+    def ex_copy(i):
         return remote(
-            eb.at[r, 0, rows(i)], eb.at[r, 1, rows(i)], ex_s.at[r, i], ex_r.at[r, i], sibling
+            eout.at[1, rows(i)], eb.at[1 - q1, 1, rows(i)], ex_s.at[i], ex_r.at[1 - q1, i],
+            (sec + toward, t ^ 1),
         )
+
+    def ex_arrived(r, i):
+        remote(
+            eout.at[r, rows(i)], eb.at[r, 1, rows(i)], ex_s.at[i], ex_r.at[r, i], sibling
+        ).wait_recv()
 
     def p_copy(r, i, m):
         return remote(
@@ -326,11 +335,10 @@
         piece = slice(i * ROWS, (i + 1) * ROWS)
         if not turn:
             ec_arrived(r, i)
-            ex_copy(r, i).start()
         e_own = eb[r, 0, piece]
         parts = [nt(e_own, weff[r, chip ^ m, :, :COLS]) for m in FAR + (0,)]
         if not turn:
-            ex_copy(r, i).wait_recv()
+            ex_arrived(r, i)
         e_other = eb[r, 1, piece]
         for m, part in zip(FAR + (0,), parts):
             part = part + nt(e_other, weff[r, chip ^ m, :, COLS:])
@@ -348,6 +356,8 @@
             total = total + pr[r, m, piece].astype(F32)
         eout[r, piece] = total.astype(BF16)
         ec_copy(r, i).start()
+        if r == 1:
+            ex_copy(i).start()
 
     def drain_backward(r):
         for i in range(SPLIT):
@@ -426,6 +436,7 @@
     def _():
         weights_here(0)
         first_layer()
+        share_weights(1)
         n_copy().start()
         share_lower(1)
         for m in FAR:
@@ -442,7 +453,7 @@
             backward_in(1, i)
         sum_g(1)
         coefficients(1)
-        drain_forward(1)
+        drain_forward(1, True)
         keep(1)
         close_backward(1)
         receive_ahead()
@@ -485,11 +496,10 @@
             backward_in(0, i)
         sum_g(0)
         close_backward(0)
-        for r in range(2):
-            for i in range(SPLIT):
-                ex_copy(r, i).wait_send()
         u_copy().wait_send()
 
+    for i in range(SPLIT):
+        ex_copy(i).wait_send()
     for r in range(2):
         c_copy(r).wait_send()
 
@@ -530,11 +540,12 @@
             pltpu.VMEM((2, CHIPS, RANK, COLS), BF16),
             pltpu.VMEM((2, 2, RANK, COLS), BF16),
             pltpu.VMEM((2, CHIPS, TOK, COLS), BF16),
-            pltpu.VMEM((2, TOK, COLS), F32),
-            pltpu.VMEM((2, TOK, COLS), F32),
             pltpu.VMEM((TOK, COLS), F32),
             pltpu.VMEM((TOK, COLS), F32),
-            pltpu.VMEM((2, TOK, COLS), BF16),
+            pltpu.VMEM((TOK, COLS), F32),
+            pltpu.VMEM((TOK, COLS), F32),
+            pltpu.VMEM((2, 2, TOK, COLS), BF16),
+            pltpu.VMEM((2, 2, TOK, COLS), BF16),
             pltpu.VMEM((2, 2, TOK, COLS), BF16),
             pltpu.VMEM((2, CHIPS, TOK, COLS), BF16),
             pltpu.VMEM((2, CHIPS, TOK, COLS), BF16),
@@ -554,8 +565,8 @@
             pltpu.VMEM((2 * CHIPS, TOK // 2, 2 * RANK), BF16),
             dma, pair, pair, pair,
             pair, pair, pair, pair, chips, chips,
-            each, each, halves, halves, halves, halves,
-            halves, halves, halves, halves,
+            each, each, dma((SPLIT,)), dma((SPLIT,)), dma((2, 2, SPLIT)), dma((2, 2, SPLIT)),
+            halves, halves, dma((SPLIT,)), halves,
             each, each, chips, chips, pair, pair,
             dma((SPLIT,)), dma((SPLIT,)), dma((CHIPS,)), dma((CHIPS,)),
             dma, dma, dma((CHIPS,)), dma((CHIPS,)), dma, dma, dma((2 * CHIPS,)), dma((2 * CHIPS,)),

time: 79.6 us -> 77.3 us (0.971)
  Pallas kernels: 78.8 us -> 76.5 us
    pallas_call x1, Pallas kernels: 77 us -> 74.6 us  [body(): pl.pallas_call(kernel, out_shape=[jax.ShapeDtypeStruct((2, TOK, n), BF16)...]
where the time goes in v4:
time: 77.3 us; the launch traced here: 77.1 us
  Pallas kernels  76.5 us (99%)
    pallas_call x1, Pallas kernels, body(): pl.pallas_call(kernel, out_shape=[jax.ShapeDtypeStruct((2, TOK, n), BF16)...  74.6 us
    pallas_call x1, Pallas kernels, body(): pl.pallas_call(gradients, out_shape=[jax.ShapeDtypeStruct((RANK, COLS), F...  1.83 us

profile of v4, /device:TPU:1, one launch (start us, length us, event | category | flops | bytes accessed | tf_op | source)
XLA Modules:
  0.0 77.1 jit_solution(5582812027780982923)
XLA Ops:
  0.6 74.6 %shard_map.111 = (bf16[2,64,64]{2,1,0:T(8,128)(2,1)}, bf16[2,64,64]{2,1,0:T(8,128)(2,1)}, bf16[2,64,256]{2,1,0:T(8,128)(2,1)}, bf16[2,64,256]{2,1,0:T(8,128)(2,1)}) custom-call(bf16[8,64,256]{2,1,0:T(8,128)(2,1)} %xd.1, bf16[8,64,256]{2,1,0:T(8,128)(2,1)} %xu.1, bf16[64,256]{1,0:T(8,128)(2,1)} %bitcast.20, bf16[64,256]{1,0:T(8,128)(2,1)} %bitcast.21, ...), custom_call_target="tpu_custom_call" | custom-call | flops 536870912 | bytes 6291456 | tf_op jit(solution)/shard_map/pallas_call | solution.py:532
  75.3 1.8 %shard_map.112 = (f32[64,256]{1,0:T(8,128)}, f32[64,256]{1,0:T(8,128)}, f32[64,256]{1,0:T(8,128)}, f32[64,256]{1,0:T(8,128)}) custom-call(bf16[2,64,64]{2,1,0:T(8,128)(2,1)} %get-tuple-element.12.c, bf16[2,64,64]{2,1,0:T(8,128)(2,1)} %get-tuple-element.13.g, bf16[2,64,256]{2,1,0:T(8,128)(2,1)} %get-tuple-element.14.h, bf16[2,64,256]{2,1,0:T(8,128)(2,1)} %get-tuple-element.15.e), custom_call_target="tpu_custom_call" | custom-call | tf_op jit(solution)/shard_map/pallas_call | solution.py:583

commit v5 on v4

--- a/solution.py
+++ b/solution.py
@@ -87,6 +87,35 @@
         for other in (t, t ^ 1):
             pl.semaphore_signal(barrier, inc=1, device_id=(sec + 1, other), device_id_type=MESH)
 
+    def every(ref, send, recv):
+        return remote(ref, ref, send, recv, sibling)
+
+    others = pl.ds(1, CHIPS - 1)
+
+    def all_h(r):
+        return every(hb.at[r, others], h_s.at[r], h_r.at[r, 0, 0])
+
+    def all_a(r):
+        return every(at.at[r, others], a_s.at[r], a_r.at[r])
+
+    def all_f():
+        return every(fr.at[others], f_s, f_r)
+
+    def all_p(r):
+        return every(ps.at[r, others], p_s.at[r], p_r.at[r, 0])
+
+    def all_p_in(r, i):
+        return every(pr.at[r, others, rows(i)], p_s.at[r], p_r.at[r, i])
+
+    def all_g(r):
+        return every(gr.at[r, others], g_s.at[r], g_r.at[r])
+
+    def all_m():
+        return every(b0.at[others], m_s, m_r)
+
+    def all_v():
+        return every(vr.at[pl.ds(1, 2 * CHIPS - 1)], v_s, v_r)
+
     def start_local(r, down):
         x, a, b, v = (xd, atd, bd, wd) if down else (xu, atu, bu, wu)
         if r == 0:
@@ -113,11 +142,11 @@
 
     def h_copy(r, i, m):
         return remote(
-            hb.at[r, 0, rows(i)], hb.at[r, m, rows(i)], h_s.at[r, i, m], h_r.at[r, i, m], peer(m)
+            hb.at[r, 0, rows(i)], hb.at[r, m, rows(i)], h_s.at[r], h_r.at[r, i, m], peer(m)
         )
 
     def a_copy(r, m):
-        return remote(at.at[r, 0], at.at[r, m], a_s.at[r, m], a_r.at[r, m], peer(m))
+        return remote(at.at[r, 0], at.at[r, m], a_s.at[r], a_r.at[r], peer(m))
 
     def b_copy(r):
         return remote(bch.at[r, 0], bch.at[r, 1], b_s.at[r], b_r.at[r], sibling)
@@ -133,7 +162,7 @@
             h_copy(0, 0, m).start()
 
     def f_copy(m):
-        return remote(fs, fr.at[m], f_s.at[m], f_r.at[m], peer(m))
+        return remote(fs, fr.at[m], f_s, f_r, peer(m))
 
     for r in range(2):
         pltpu.make_async_copy(atd, at.at[r, 0], ld_a.at[r]).wait()
@@ -177,9 +206,8 @@
         w_copy(r, True).wait_recv()
 
     def combine_weights(r):
+        all_a(r).wait_recv()
         for m in NEAR:
-            if m:
-                a_copy(r, m).wait_recv()
             j = chip ^ m
             for half in range(2):
                 low_rank = tn(at[r, m], bch[r, half])
@@ -232,8 +260,8 @@
                 other = other + nn(hb[0, m, piece], w[0, 1, chip ^ m])
             if i == 0:
                 lower = fs[...]
+                all_f().wait_recv()
                 for m in NEAR[1:]:
-                    f_copy(m).wait_recv()
                     lower = lower + fr[m]
                 cs[0] = lower
                 c = unfold(lower).astype(BF16)
@@ -277,9 +305,8 @@
         c_copy(r).start()
 
     def drain_forward(r, last=False):
-        for i in range(SPLIT):
-            for m in FAR:
-                h_copy(r, i, m).wait_send()
+        all_h(r).wait_send()
+        for i in range(SPLIT):
             if last:
                 hx_copy(i).wait_send()
                 t_copy(i).wait_send()
@@ -289,8 +316,7 @@
 
     def drain_weights(r):
         if r == 1:
-            for m in FAR:
-                a_copy(r, m).wait_send()
+            all_a(r).wait_send()
         b_copy(r).wait_send()
         w_copy(r, True).wait_send()
 
@@ -319,11 +345,11 @@
 
     def p_copy(r, i, m):
         return remote(
-            ps.at[r, m, rows(i)], pr.at[r, m, rows(i)], p_s.at[r, i, m], p_r.at[r, i, m], peer(m)
+            ps.at[r, m, rows(i)], pr.at[r, m, rows(i)], p_s.at[r], p_r.at[r, i], peer(m)
         )
 
     def g_copy(r, m):
-        return remote(gs.at[r], gr.at[r, m], g_s.at[r, m], g_r.at[r, m], peer(m))
+        return remote(gs.at[r], gr.at[r, m], g_s.at[r], g_r.at[r], peer(m))
 
     def sum_g(r):
         total = nt(eb[r, 0], bch[r, 0]) + nt(eb[r, 1], bch[r, 1])
@@ -351,8 +377,8 @@
     def backward_in(r, i):
         piece = slice(i * ROWS, (i + 1) * ROWS)
         total = kept[r, piece]
+        all_p_in(r, i).wait_recv()
         for m in NEAR[1:]:
-            p_copy(r, i, m).wait_recv()
             total = total + pr[r, m, piece].astype(F32)
         eout[r, piece] = total.astype(BF16)
         ec_copy(r, i).start()
@@ -360,37 +386,34 @@
             ex_copy(i).start()
 
     def drain_backward(r):
-        for i in range(SPLIT):
-            for m in FAR:
-                p_copy(r, i, m).wait_send()
+        all_p(r).wait_send()
+        for i in range(SPLIT):
             ec_copy(r, i).wait_send()
 
     def n_copy():
         return remote(bch.at[0, 0], b0.at[0], n_s, n_r, (sec + toward, t))
 
     def m_copy(m):
-        return remote(b0.at[0], b0.at[m], m_s.at[m], m_r.at[m], peer(m))
+        return remote(b0.at[0], b0.at[m], m_s, m_r, peer(m))
 
     def u_copy():
         return remote(us, ur, u_s, u_r, (sec - toward, t))
 
     def v_copy(n):
-        return remote(vs, vr.at[n], v_s.at[n], v_r.at[n], (sec, t ^ n))
+        return remote(vs, vr.at[n], v_s, v_r, (sec, t ^ n))
 
     def prepare_ahead():
         remote(bch.at[0, 0], b0.at[0], n_s, n_r, sibling).wait_recv()
         for m in FAR:
             m_copy(m).start()
         own, other = b0[0].astype(F32), jnp.zeros((RANK, COLS), F32)
+        all_m().wait_recv()
         for m in NEAR:
-            if m:
-                m_copy(m).wait_recv()
             own = own + nn(b0[m], weff[0, chip ^ m, :, :COLS])
             other = other + nn(b0[m], weff[0, chip ^ m, :, COLS:])
         bp[0] = own.astype(BF16)
         bp[1] = other.astype(BF16)
-        for m in FAR:
-            m_copy(m).wait_send()
+        all_m().wait_send()
 
     def send_ahead():
         us[...] = fold(nt(eb[0, 0], bp[0]) + nt(eb[0, 1], bp[1]))
@@ -402,8 +425,8 @@
         for n in WIDE:
             v_copy(n).start()
         total = ur[...]
+        all_v().wait_recv()
         for n in reversed(WIDE):
-            v_copy(n).wait_recv()
             total = total + vr[n].astype(F32)
         g_out[0] = unfold(total).astype(BF16)
 
@@ -414,8 +437,8 @@
 
     def finish(r):
         total = gs[r]
+        all_g(r).wait_recv()
         for m in NEAR[1:]:
-            g_copy(r, m).wait_recv()
             total = total + gr[r, m]
         g_out[r] = unfold(total).astype(BF16)
         e_out[r] = eb[r, 0]
@@ -429,8 +452,7 @@
     def close_backward(r):
         finish(r)
         drain_backward(r)
-        for m in FAR:
-            g_copy(r, m).wait_send()
+        all_g(r).wait_send()
 
     @pl.when(q1 == 0)
     def _():
@@ -439,8 +461,7 @@
         share_weights(1)
         n_copy().start()
         share_lower(1)
-        for m in FAR:
-            f_copy(m).wait_send()
+        all_f().wait_send()
         weights_here(1)
         combine_weights(1)
         n_copy().wait_send()
@@ -457,8 +478,7 @@
         keep(1)
         close_backward(1)
         receive_ahead()
-        for n in WIDE:
-            v_copy(n).wait_send()
+        all_v().wait_send()
         for i in range(SPLIT):
             ec_arrived(0, i)
         e_out[0] = eb[0, 0]
@@ -474,8 +494,7 @@
             later_layer(0, i, False)
         gather(1)
         coefficients(0)
-        for m in FAR:
-            a_copy(0, m).wait_send()
+        all_a(0).wait_send()
         close_forward()
         for i in range(SPLIT):
             later_layer(1, i, False)
@@ -528,7 +547,6 @@
     pair = dma((2,))
     halves = dma((2, SPLIT))
     each = dma((2, SPLIT, CHIPS))
-    chips = dma((2, CHIPS))
     parts = pl.pallas_call(
         kernel,
         out_shape=[jax.ShapeDtypeStruct((2, TOK, n), BF16) for n in (RANK, RANK, COLS, COLS)],
@@ -564,12 +582,12 @@
             pltpu.VMEM((TOK // 2, 2 * RANK), BF16),
             pltpu.VMEM((2 * CHIPS, TOK // 2, 2 * RANK), BF16),
             dma, pair, pair, pair,
-            pair, pair, pair, pair, chips, chips,
-            each, each, dma((SPLIT,)), dma((SPLIT,)), dma((2, 2, SPLIT)), dma((2, 2, SPLIT)),
+            pair, pair, pair, pair, pair, pair,
+            pair, each, dma((SPLIT,)), dma((SPLIT,)), dma((2, 2, SPLIT)), dma((2, 2, SPLIT)),
             halves, halves, dma((SPLIT,)), halves,
-            each, each, chips, chips, pair, pair,
-            dma((SPLIT,)), dma((SPLIT,)), dma((CHIPS,)), dma((CHIPS,)),
-            dma, dma, dma((CHIPS,)), dma((CHIPS,)), dma, dma, dma((2 * CHIPS,)), dma((2 * CHIPS,)),
+            pair, halves, pair, pair, pair, pair,
+            dma((SPLIT,)), dma((SPLIT,)), dma, dma,
+            dma, dma, dma, dma, dma, dma, dma, dma,
         ],
         compiler_params=pltpu.CompilerParams(
             collective_id=0, has_side_effects=True, vmem_limit_bytes=62 * 2**20

time: 77.3 us -> 75.5 us (0.977)
  Pallas kernels: 76.5 us -> 74.6 us
    pallas_call x1, Pallas kernels: 74.6 us -> 72.8 us  [body(): pl.pallas_call(kernel, out_shape=[jax.ShapeDtypeStruct((2, TOK, n), BF16)...]
where the time goes in v5:
time: 75.5 us; the launch traced here: 75.3 us
  Pallas kernels  74.6 us (99%)
    pallas_call x1, Pallas kernels, body(): pl.pallas_call(kernel, out_shape=[jax.ShapeDtypeStruct((2, TOK, n), BF16)...  72.8 us
    pallas_call x1, Pallas kernels, body(): pl.pallas_call(gradients, out_shape=[jax.ShapeDtypeStruct((RANK, COLS), F...  1.83 us

profile of v5, /device:TPU:1, one launch (start us, length us, event | category | flops | bytes accessed | tf_op | source)
XLA Modules:
  0.0 75.3 jit_solution(132669563690558051)
XLA Ops:
  0.6 72.8 %shard_map.111 = (bf16[2,64,64]{2,1,0:T(8,128)(2,1)}, bf16[2,64,64]{2,1,0:T(8,128)(2,1)}, bf16[2,64,256]{2,1,0:T(8,128)(2,1)}, bf16[2,64,256]{2,1,0:T(8,128)(2,1)}) custom-call(bf16[8,64,256]{2,1,0:T(8,128)(2,1)} %xd.1, bf16[8,64,256]{2,1,0:T(8,128)(2,1)} %xu.1, bf16[64,256]{1,0:T(8,128)(2,1)} %bitcast.20, bf16[64,256]{1,0:T(8,128)(2,1)} %bitcast.21, ...), custom_call_target="tpu_custom_call" | custom-call | flops 536870912 | bytes 6291456 | tf_op jit(solution)/shard_map/pallas_call | solution.py:550
  73.4 1.8 %shard_map.112 = (f32[64,256]{1,0:T(8,128)}, f32[64,256]{1,0:T(8,128)}, f32[64,256]{1,0:T(8,128)}, f32[64,256]{1,0:T(8,128)}) custom-call(bf16[2,64,64]{2,1,0:T(8,128)(2,1)} %get-tuple-element.12.c, bf16[2,64,64]{2,1,0:T(8,128)(2,1)} %get-tuple-element.13.g, bf16[2,64,256]{2,1,0:T(8,128)(2,1)} %get-tuple-element.14.h, bf16[2,64,256]{2,1,0:T(8,128)(2,1)} %get-tuple-element.15.e), custom_call_target="tpu_custom_call" | custom-call | tf_op jit(solution)/shard_map/pallas_call | solution.py:601

commit v6 on v5

--- a/solution.py
+++ b/solution.py
@@ -45,7 +45,7 @@
 def kernel(
     xd, xu, atd, atu, bd, bu, wd, wu,
     c_out, g_out, h_out, e_out,
-    w, weff, at, bch, hb, xs, xp, ts, tp, hs, hin, eb, ps, pr, eout, gs, gr, cs, cr, fs, fr,
+    w, weff, weft, at, bch, hb, xs, xp, ts, tp, hs, hin, eb, ps, pr, eout, gs, gr, cs, cr, fs, fr,
     kept, b0, bp, us, ur, vs, vr,
     ld_x, ld_a, ld_b, ld_w,
     w_s, w_r, b_s, b_r, a_s, a_r, h_s, h_r, hx_s, hx_r, hc_s, hc_r,
@@ -223,15 +223,12 @@
         there = q1 if r == 0 else 1
         return remote(
             hs.at[r, half, rows(i)], hin.at[there, half, rows(i)],
-            hc_s.at[r, half, i], hc_r.at[there, half, i], to,
+            hc_s.at[r], hc_r.at[there, i], to,
         )
 
     def hc_arrived(r, i):
-        for half in range(2):
-            remote(
-                hs.at[r, half, rows(i)], hin.at[r, half, rows(i)],
-                hc_s.at[r, half, i], hc_r.at[r, half, i], sibling,
-            ).wait_recv()
+        arrived = hin.at[r, :, rows(i)]
+        every(arrived, hc_s.at[r], hc_r.at[r, i]).wait_recv()
         piece = slice(i * ROWS, (i + 1) * ROWS)
         hb[r, 0, piece] = (
             hin[r, 0, piece].astype(F32) + hin[r, 1, piece].astype(F32)
@@ -306,13 +303,12 @@
 
     def drain_forward(r, last=False):
         all_h(r).wait_send()
-        for i in range(SPLIT):
-            if last:
+        if last:
+            for i in range(SPLIT):
                 hx_copy(i).wait_send()
                 t_copy(i).wait_send()
-            else:
-                for half in range(2):
-                    hc_copy(r, i, half).wait_send()
+        else:
+            every(hs.at[r], hc_s.at[r], hc_r.at[r, 0]).wait_send()
 
     def drain_weights(r):
         if r == 1:
@@ -362,12 +358,12 @@
         if not turn:
             ec_arrived(r, i)
         e_own = eb[r, 0, piece]
-        parts = [nt(e_own, weff[r, chip ^ m, :, :COLS]) for m in FAR + (0,)]
+        parts = [nn(e_own, weft[r, chip ^ m, :COLS]) for m in FAR + (0,)]
         if not turn:
             ex_arrived(r, i)
         e_other = eb[r, 1, piece]
         for m, part in zip(FAR + (0,), parts):
-            part = part + nt(e_other, weff[r, chip ^ m, :, COLS:])
+            part = part + nn(e_other, weft[r, chip ^ m, COLS:])
             if m:
                 ps[r, m, piece] = part.astype(BF16)
                 p_copy(r, i, m).start()
@@ -401,6 +397,13 @@
 
     def v_copy(n):
         return remote(vs, vr.at[n], v_s, v_r, (sec, t ^ n))
+
+    def transpose_weights(r):
+        def one(j, _):
+            weft[r, j] = weff[r, j].T
+            return 0
+
+        lax.fori_loop(0, CHIPS, one, 0)
 
     def prepare_ahead():
         remote(bch.at[0, 0], b0.at[0], n_s, n_r, sibling).wait_recv()
@@ -464,6 +467,7 @@
         all_f().wait_send()
         weights_here(1)
         combine_weights(1)
+        transpose_weights(1)
         n_copy().wait_send()
         close_forward()
         gather(1)
@@ -499,6 +503,8 @@
         for i in range(SPLIT):
             later_layer(1, i, False)
         prepare_ahead()
+        transpose_weights(1)
+        transpose_weights(0)
         coefficients(1)
         drain_forward(1)
         keep(1)
@@ -555,6 +561,7 @@
         scratch_shapes=[
             pltpu.VMEM((2, 2, CHIPS, COLS, COLS), BF16),
             pltpu.VMEM((2, CHIPS, COLS, 2 * COLS), BF16),
+            pltpu.VMEM((2, CHIPS, 2 * COLS, COLS), BF16),
             pltpu.VMEM((2, CHIPS, RANK, COLS), BF16),
             pltpu.VMEM((2, 2, RANK, COLS), BF16),
             pltpu.VMEM((2, CHIPS, TOK, COLS), BF16),
@@ -583,7 +590,7 @@
             pltpu.VMEM((2 * CHIPS, TOK // 2, 2 * RANK), BF16),
             dma, pair, pair, pair,
             pair, pair, pair, pair, pair, pair,
-            pair, each, dma((SPLIT,)), dma((SPLIT,)), dma((2, 2, SPLIT)), dma((2, 2, SPLIT)),
+            pair, each, dma((SPLIT,)), dma((SPLIT,)), pair, halves,
             halves, halves, dma((SPLIT,)), halves,
             pair, halves, pair, pair, pair, pair,
             dma((SPLIT,)), dma((SPLIT,)), dma, dma,

time: 75.5 us -> 73.7 us (0.976)
  Pallas kernels: 74.6 us -> 72.9 us
    pallas_call x1, Pallas kernels: 72.8 us -> 71.1 us  [body(): pl.pallas_call(kernel, out_shape=[jax.ShapeDtypeStruct((2, TOK, n), BF16)...]
where the time goes in v6:
time: 73.7 us; the launch traced here: 73.5 us
  Pallas kernels  72.9 us (99%)
    pallas_call x1, Pallas kernels, body(): pl.pallas_call(kernel, out_shape=[jax.ShapeDtypeStruct((2, TOK, n), BF16)...  71.1 us
    pallas_call x1, Pallas kernels, body(): pl.pallas_call(gradients, out_shape=[jax.ShapeDtypeStruct((RANK, COLS), F...  1.83 us

profile of v6, /device:TPU:1, one launch (start us, length us, event | category | flops | bytes accessed | tf_op | source)
XLA Modules:
  0.0 73.5 jit_solution(18443557640782254430)
XLA Ops:
  0.6 71.1 %shard_map.111 = (bf16[2,64,64]{2,1,0:T(8,128)(2,1)}, bf16[2,64,64]{2,1,0:T(8,128)(2,1)}, bf16[2,64,256]{2,1,0:T(8,128)(2,1)}, bf16[2,64,256]{2,1,0:T(8,128)(2,1)}) custom-call(bf16[8,64,256]{2,1,0:T(8,128)(2,1)} %xd.1, bf16[8,64,256]{2,1,0:T(8,128)(2,1)} %xu.1, bf16[64,256]{1,0:T(8,128)(2,1)} %bitcast.20, bf16[64,256]{1,0:T(8,128)(2,1)} %bitcast.21, ...), custom_call_target="tpu_custom_call" | custom-call | flops 536870912 | bytes 6291456 | tf_op jit(solution)/shard_map/pallas_call | solution.py:556
  71.7 1.8 %shard_map.112 = (f32[64,256]{1,0:T(8,128)}, f32[64,256]{1,0:T(8,128)}, f32[64,256]{1,0:T(8,128)}, f32[64,256]{1,0:T(8,128)}) custom-call(bf16[2,64,64]{2,1,0:T(8,128)(2,1)} %get-tuple-element.12.c, bf16[2,64,64]{2,1,0:T(8,128)(2,1)} %get-tuple-element.13.g, bf16[2,64,256]{2,1,0:T(8,128)(2,1)} %get-tuple-element.14.h, bf16[2,64,256]{2,1,0:T(8,128)(2,1)} %get-tuple-element.15.e), custom_call_target="tpu_custom_call" | custom-call | tf_op jit(solution)/shard_map/pallas_call | solution.py:608
